TPU v7x, 128 devices: a whole 4x4x4 slice. The times are simulated.
128 devices in a mesh: stream: 8 (over x_lo, y), cross: 16 (over z, x_hi, core).
Axes of the slice: x: 4 (x_hi: 2, x_lo: 2; x = x_hi * 2 + x_lo), y: 4, z: 4, core: 2. Of those that a mesh axis runs over, the one named last changes fastest.
Arguments:
- basis: bfloat16 [786432, 256], P(('stream', 'cross')), may hold values from -24 to 24
- volume: float32 [786432], P(('stream', 'cross')), may hold values from 0.3 to 3
- own_blocks: bfloat16 [12288, 7, 64, 128], P(('stream', 'cross')), may hold values from -0.25 to 0.25
- own_cols: int32 [12288, 7], P(('stream', 'cross')), may hold values from 0 to 95
- border_blocks: bfloat16 [128, 4, 8, 64, 128], P(('stream', 'cross')), may hold values from -0.25 to 0.25
- border_cols: int32 [128, 4, 8], P(('stream', 'cross')), may hold values from 0 to 95
- border_rows: int32 [128, 4, 8], P(('stream', 'cross')), may hold values from 0 to 95
Outputs:
- applied_basis: bfloat16 [2, 786432, 256], P(None, ('stream', 'cross'))
- reduced_operator: float32 [256, 2, 256], P(('stream', 'cross'))
Inputs may be any that keep to these rules, and one draw needn't show every extreme that they name: `own_cols`: block indices within the device's own tile. `border_cols`: block indices within the sending tile. `border_rows`: block rows within the receiving neighbour's tile.
All inputs are finite; a program needn't handle non-finite values.
Results may differ from a plain program's by a relative error of at most 0.003.
Values may be sent and summed in bfloat16 or wider, within the bound.
A program may use at most 128 MiB of HBM per device.

v0:
```python
import math

import jax
import jax.numpy as jnp
from jax import lax
from jax.sharding import PartitionSpec as P


def passed_along(value, axis, steps):
    count = lax.axis_size(axis)
    leading, last = (max(0, -steps), min(count, count - steps))
    return lax.ppermute(value, axis, [(source, source + steps) for source in range(leading, last)])


def local(basis, volume, own_blocks, own_cols, border_blocks, border_cols, border_rows):
    mode_count = basis.shape[1]
    block_size = own_blocks.shape[2]
    block_count = own_cols.shape[0]
    stream_count = lax.axis_size("stream")
    cross_count = lax.axis_size("cross")
    basis_blocks = basis.reshape(block_count, block_size, mode_count)
    gathered = basis_blocks[own_cols]
    applied = jnp.einsum("bkcr,bkcm->brm", own_blocks, gathered, preferred_element_type=jnp.float32)
    edge_blocks = border_blocks[0]
    edge_sources = basis_blocks[border_cols[0]]
    edge_targets = border_rows[0]
    partial_rows = jnp.einsum(
        "dncr,dncm->dnrm", edge_blocks, edge_sources, preferred_element_type=jnp.float32
    )
    received = [
        (
            passed_along(partial_rows[0].astype(jnp.bfloat16), "stream", 1).astype(jnp.float32),
            passed_along(edge_targets[0], "stream", 1),
        ),
        (
            passed_along(partial_rows[1].astype(jnp.bfloat16), "stream", -1).astype(jnp.float32),
            passed_along(edge_targets[1], "stream", -1),
        ),
        (
            passed_along(partial_rows[2].astype(jnp.bfloat16), "cross", 1).astype(jnp.float32),
            passed_along(edge_targets[2], "cross", 1),
        ),
        (
            passed_along(partial_rows[3].astype(jnp.bfloat16), "cross", -1).astype(jnp.float32),
            passed_along(edge_targets[3], "cross", -1),
        ),
    ]
    incoming = jnp.concatenate([item[0] for item in received], axis=0)
    targets = jnp.concatenate([item[1] for item in received], axis=0)
    applied = applied.at[targets].add(incoming)
    split = applied.reshape(block_count, 2, block_size, mode_count)
    applied_basis = (
        split.transpose(1, 0, 2, 3)
        .reshape(2, block_count * block_size, mode_count)
        .astype(jnp.bfloat16)
    )
    norm_factor = 1.0 / math.sqrt(stream_count * cross_count * block_count * block_size)
    weighted = (split * volume.reshape(block_count, 1, block_size, 1) * norm_factor).astype(
        jnp.bfloat16
    )
    reduced = lax.psum_scatter(
        jnp.einsum("bca,btcm->atm", basis_blocks, weighted, preferred_element_type=jnp.float32),
        ("stream", "cross"),
        scatter_dimension=0,
        tiled=True,
    )
    return (applied_basis, reduced)


def solution(mesh):
    return jax.shard_map(
        local,
        mesh=mesh,
        in_specs=(
            P(("stream", "cross"), None),
            P(("stream", "cross")),
            P(("stream", "cross"), None, None, None),
            P(("stream", "cross"), None),
            P(("stream", "cross"), None, None, None, None),
            P(("stream", "cross"), None, None),
            P(("stream", "cross"), None, None),
        ),
        out_specs=(P(None, ("stream", "cross"), None), P(("stream", "cross"), None, None)),
        check_vma=False,
    )
```

profile of v0, /device:TPU:0, one launch (start us, length us, event | category | flops | bytes accessed | tf_op | source)
XLA Modules:
  0.0 291.5 jit_solution(3078198336214135197)
XLA Ops:
  7.2 0.0 copy-start
  7.2 0.0 copy-start.2
  7.2 0.0 all-reduce.3.cloned.1.call-start
  7.2 0.9 slice_bitcast_fusion.7
  8.1 1.4 collective-permute-start.3
  9.5 0.7 compare_select_fusion.1
  10.2 0.1 reshape.223
  10.3 0.0 copy-done
  10.3 1.6 gather_fusion.1
  11.9 2.1 convert_bitcast_fusion
  14.0 1.4 slice_bitcast_fusion.3
  15.4 1.3 collective-permute-start.7
  16.7 4.5 %collective-permute-start.6 = (bf16[8,128,256]{1,2,0:T(8,128)(2,1)}, bf16[8,128,256]{1,2,0:T(8,128)(2,1)}, u32[]{:S(2)}, u32[]{:S(2)}) collective-permute-start(bf16[8,128,256]{1,2,0:T(8,128)(2,1)} %get-tuple-element.10), channel_id=1, source_target_pairs={{0,1},{1,2},{2,3},{3,4},{4,5},{5,6},{6,7},{7,8},{8,9},{9,10},{10,1... | collective-permute-start | bytes 1572872 | tf_op jit(solution)/shard_map/ppermute | solution.py:12
  21.2 1.3 collective-permute-start.5
  22.5 5.4 %collective-permute-start.4 = (bf16[8,128,256]{1,2,0:T(8,128)(2,1)}, bf16[8,128,256]{1,2,0:T(8,128)(2,1)}, u32[]{:S(2)}, u32[]{:S(2)}) collective-permute-start(bf16[8,128,256]{1,2,0:T(8,128)(2,1)} %get-tuple-element.8), channel_id=1, source_target_pairs={{0,16},{16,32},{32,48},{48,64},{64,80},{80,96},{96,112},{1,17},{17... | collective-permute-start | bytes 1572872 | tf_op jit(solution)/shard_map/ppermute | solution.py:12
  27.8 0.0 copy-done.2
  27.8 0.1 copy.24
  27.9 0.2 reshape.215
  28.1 18.3 %gather_fusion = bf16[672,64,256]{2,1,0:T(8,128)(2,1)} fusion(bf16[96,64,256]{2,1,0:T(8,128)(2,1)S(1)} %bitcast.58, s32[1024]{0:T(1024)S(1)} %pad_clamp_fusion.1), kind=kCustom, calls=%fused_computation | custom fusion | bytes 44042880 | tf_op jit(solution)/shard_map/gather | solution.py:22
  46.4 18.3 %convolution_bitcast_fusion = f32[96,128,256]{1,2,0:T(8,128)} fusion(bf16[96,7,64,256]{3,2,1,0:T(8,128)(2,1)} %bitcast.61, bf16[96,7,64,128]{3,2,1,0:T(8,128)(2,1)} %param.9), kind=kOutput, calls=%fused_computation.4 | convolution fusion | flops 2818572288 | bytes 45613056 | tf_op jit(solution)/shard_map/bkcr,bkcm->brm/dot_general | solution.py:23
  64.7 0.0 copy-start.1
  64.7 12.6 %copy.25 = f32[96,128,256]{2,1,0:T(8,128)} copy(f32[96,128,256]{1,2,0:T(8,128)} %convolution_bitcast_fusion) | data formatting | bytes 25165824 | tf_op jit(solution)/shard_map/bkcr,bkcm->brm/dot_general | solution.py:23
  77.3 0.0 copy-done.1
  77.3 0.1 mul.22
  77.3 0.1 copy.28
  77.4 0.1 copy.29
  77.5 0.0 collective-permute-done.3
  77.5 3.8 %collective-permute-start.2 = (s32[8]{0:T(128)S(1)}, s32[8]{0:T(128)S(1)}, u32[]{:S(2)}, u32[]{:S(2)}) collective-permute-start(s32[8]{0:T(128)S(1)} %get-tuple-element.15), channel_id=1, source_target_pairs={{0,1},{1,2},{2,3},{3,4},{4,5},{5,6},{6,7},{7,8},{8,9},{9,10},{10,1... | collective-permute-start | bytes 104 | tf_op jit(solution)/shard_map/ppermute | solution.py:12
  81.3 0.8 collective-permute-done.2
  82.1 1.3 collective-permute-start.1
  83.4 4.1 %collective-permute-done.1 = s32[8]{0:T(128)S(1)} collective-permute-done((s32[8]{0:T(128)S(1)}, s32[8]{0:T(128)S(1)}, u32[]{:S(2)}, u32[]{:S(2)}) %collective-permute-start.1) | collective-permute-done | bytes 64 | tf_op jit(solution)/shard_map/ppermute | solution.py:12
  87.5 3.0 %collective-permute-start = (s32[8]{0:T(128)S(1)}, s32[8]{0:T(128)S(1)}, u32[]{:S(2)}, u32[]{:S(2)}) collective-permute-start(s32[8]{0:T(128)S(1)} %get-tuple-element.12), channel_id=1, source_target_pairs={{0,16},{16,32},{32,48},{48,64},{64,80},{80,96},{96,112},{1,17},{17... | collective-permute-start | bytes 104 | tf_op jit(solution)/shard_map/ppermute | solution.py:12
  90.5 1.1 collective-permute-done
  91.6 0.1 fusion.1
  91.7 0.0 collective-permute-done.7
  91.7 0.0 collective-permute-done.6
  91.7 0.0 collective-permute-done.5
  91.7 0.0 collective-permute-done.4
  91.7 3.9 %maximum_convert_fusion = f32[32,128,256]{1,2,0:T(8,128)} fusion(bf16[8,128,256]{1,2,0:T(8,128)(2,1)} %collective-permute-done.7, bf16[8,128,256]{1,2,0:T(8,128)(2,1)} %collective-permute-done.6, bf16[8,128,256]{1,2,0:T(8,128)(2,1)} %collective-permute-done.5, bf16[8,128,256]{1,2,0:T(8,128)(2,1)} %collective-permute-done.4), kind=kLoop, calls=%fused_computation.5 | loop fusion | flops 4194304 | bytes 6291456 | tf_op jit(solution)/shard_map/concatenate | solution.py:48
  95.6 5.6 %copy.26 = f32[32,128,256]{2,1,0:T(8,128)} copy(f32[32,128,256]{1,2,0:T(8,128)} %maximum_convert_fusion) | data formatting | bytes 8388608 | tf_op jit(solution)/shard_map/concatenate | solution.py:48
  101.2 9.7 %scatter_fusion = f32[96,128,256]{2,1,0:T(8,128)} fusion(f32[96,128,256]{2,1,0:T(8,128)} %copy.25, s32[32]{0:T(128)S(1)} %fusion.1, f32[32,128,256]{2,1,0:T(8,128)} %copy.26), kind=kCustom, calls=%fused_computation.2 | custom fusion | flops 1048576 | bytes 12583040 | tf_op jit(solution)/shard_map/scatter-add | solution.py:50
  110.9 13.7 %multiply_convert_fusion = (bf16[96,128,256]{2,1,0:T(8,128)(2,1)S(1)}, bf16[96,128,256]{2,1,0:T(8,128)(2,1)}) fusion(f32[96,128,256]{2,1,0:T(8,128)} %scatter_fusion, f32[96,128]{1,0:T(8,128)S(1)} %copy.29), kind=kLoop, calls=%fused_computation.3 | loop fusion | flops 12582912 | bytes 25214976 | tf_op jit(solution)/shard_map/convert_element_type | solution.py:58
  124.6 2.6 convolution_bitcast_fusion.1
  127.3 2.0 copy.30
  129.3 0.0 all-reduce.3.cloned.1.call-update
  129.3 6.6 %copy.27 = bf16[2,96,64,256]{3,2,1,0:T(8,128)(2,1)} copy(bf16[2,96,64,256]{3,2,0,1:T(8,128)(2,1)} %bitcast.63) | data formatting | bytes 12582912 | tf_op jit(solution)/shard_map/convert_element_type | solution.py:55
  135.9 147.5 %all-reduce.3.cloned.1.call-done = f32[256,2,256]{2,1,0:T(2,128)} async-done(((f32[256,2,256]{2,1,0:T(2,128)}), f32[256,2,256]{2,1,0:T(2,128)}) %all-reduce.3.cloned.1.call-update) | async-done | bytes 524304
  283.4 1.3 constant_dynamic-slice_fusion
  (4 shorter events, 0.0 us)
Async XLA Ops:
  7.2 3.2 %copy-start = (bf16[6144,256]{1,0:T(8,128)(2,1)S(1)}, bf16[6144,256]{1,0:T(8,128)(2,1)}, u32[]{:S(2)}) copy-start(bf16[6144,256]{1,0:T(8,128)(2,1)} %param.7) | copy-start | bytes 9437188
  7.2 20.6 %copy-start.2 = (s32[96,7]{0,1:T(8,128)S(1)}, s32[96,7]{0,1:T(8,128)}, u32[]{:S(2)}) copy-start(s32[96,7]{0,1:T(8,128)} %param.10) | copy-start | bytes 8068
  7.2 276.2 %all-reduce.3.cloned.1.call-start = ((), (), s32[]{:S(2)}) async-start(), calls=%async_computation | async-start | bytes 1048576
  8.1 69.4 %collective-permute-start.3 = (s32[8]{0:T(128)S(1)}, s32[8]{0:T(128)S(1)}, u32[]{:S(2)}, u32[]{:S(2)}) collective-permute-start(s32[8]{0:T(128)S(1)} %get-tuple-element.14), channel_id=1, source_target_pairs={{1,0},{2,1},{3,2},{4,3},{5,4},{6,5},{7,6},{8,7},{9,8},{10,9},{11,1... | collective-permute-start | bytes 104 | tf_op jit(solution)/shard_map/ppermute | solution.py:12
  15.4 76.3 %collective-permute-start.7 = (bf16[8,128,256]{1,2,0:T(8,128)(2,1)}, bf16[8,128,256]{1,2,0:T(8,128)(2,1)}, u32[]{:S(2)}, u32[]{:S(2)}) collective-permute-start(bf16[8,128,256]{1,2,0:T(8,128)(2,1)} %get-tuple-element.9), channel_id=1, source_target_pairs={{1,0},{2,1},{3,2},{4,3},{5,4},{6,5},{7,6},{8,7},{9,8},{10,9},{11,1... | collective-permute-start | bytes 1572872 | tf_op jit(solution)/shard_map/ppermute | solution.py:12
  16.7 75.0 %collective-permute-start.6 = (bf16[8,128,256]{1,2,0:T(8,128)(2,1)}, bf16[8,128,256]{1,2,0:T(8,128)(2,1)}, u32[]{:S(2)}, u32[]{:S(2)}) collective-permute-start(bf16[8,128,256]{1,2,0:T(8,128)(2,1)} %get-tuple-element.10), channel_id=1, source_target_pairs={{0,1},{1,2},{2,3},{3,4},{4,5},{5,6},{6,7},{7,8},{8,9},{9,10},{10,1... | collective-permute-start | bytes 1572872 | tf_op jit(solution)/shard_map/ppermute | solution.py:12
  21.2 70.5 %collective-permute-start.5 = (bf16[8,128,256]{1,2,0:T(8,128)(2,1)}, bf16[8,128,256]{1,2,0:T(8,128)(2,1)}, u32[]{:S(2)}, u32[]{:S(2)}) collective-permute-start(bf16[8,128,256]{1,2,0:T(8,128)(2,1)} %get-tuple-element.11), channel_id=1, source_target_pairs={{16,0},{32,16},{48,32},{64,48},{80,64},{96,80},{112,96},{17,1},{33... | collective-permute-start | bytes 1572872 | tf_op jit(solution)/shard_map/ppermute | solution.py:12
  22.5 69.2 %collective-permute-start.4 = (bf16[8,128,256]{1,2,0:T(8,128)(2,1)}, bf16[8,128,256]{1,2,0:T(8,128)(2,1)}, u32[]{:S(2)}, u32[]{:S(2)}) collective-permute-start(bf16[8,128,256]{1,2,0:T(8,128)(2,1)} %get-tuple-element.8), channel_id=1, source_target_pairs={{0,16},{16,32},{32,48},{48,64},{64,80},{80,96},{96,112},{1,17},{17... | collective-permute-start | bytes 1572872 | tf_op jit(solution)/shard_map/ppermute | solution.py:12
  64.7 12.6 %copy-start.1 = (f32[6144]{0:T(1024)S(1)}, f32[6144]{0:T(1024)}, u32[]{:S(2)}) copy-start(f32[6144]{0:T(1024)} %param.8) | copy-start | bytes 73732
  77.5 4.6 %collective-permute-start.2 = (s32[8]{0:T(128)S(1)}, s32[8]{0:T(128)S(1)}, u32[]{:S(2)}, u32[]{:S(2)}) collective-permute-start(s32[8]{0:T(128)S(1)} %get-tuple-element.15), channel_id=1, source_target_pairs={{0,1},{1,2},{2,3},{3,4},{4,5},{5,6},{6,7},{7,8},{8,9},{9,10},{10,1... | collective-permute-start | bytes 104 | tf_op jit(solution)/shard_map/ppermute | solution.py:12
  82.1 5.4 %collective-permute-start.1 = (s32[8]{0:T(128)S(1)}, s32[8]{0:T(128)S(1)}, u32[]{:S(2)}, u32[]{:S(2)}) collective-permute-start(s32[8]{0:T(128)S(1)} %get-tuple-element.13), channel_id=1, source_target_pairs={{16,0},{32,16},{48,32},{64,48},{80,64},{96,80},{112,96},{17,1},{33... | collective-permute-start | bytes 104 | tf_op jit(solution)/shard_map/ppermute | solution.py:12
  87.5 4.1 %collective-permute-start = (s32[8]{0:T(128)S(1)}, s32[8]{0:T(128)S(1)}, u32[]{:S(2)}, u32[]{:S(2)}) collective-permute-start(s32[8]{0:T(128)S(1)} %get-tuple-element.12), channel_id=1, source_target_pairs={{0,16},{16,32},{32,48},{48,64},{64,80},{80,96},{96,112},{1,17},{17... | collective-permute-start | bytes 104 | tf_op jit(solution)/shard_map/ppermute | solution.py:12
Sparse Core Ops, SparseCore 0:
  129.4 153.9 all-reduce.2
where the time goes:
time: 294 us; the launch traced here: 292 us
  waiting for transfers between devices  154 us (52%)
  local copies, waits for them, and re-layouts  50.8 us (17%)
  other arithmetic  28.1 us (10%)
  matrix products  23 us (8%)
  starting transfers between devices  21.9 us (7%)
  between operations  14.2 us (5%)
    unnamed x2, waiting for transfers between devices  147 us
    ppermute x8, starting transfers between devices, passed_along(): lax.ppermute(value, axis, [(source, source + steps) for source in range(l...  21.8 us
    dot_general x1, matrix products, local(): jnp.einsum('bkcr,bkcm->brm', own_blocks, gathered, preferred_element_type...  18.3 us
    gather x1, local copies, waits for them, and re-layouts, local(): gathered = basis_blocks[own_cols]  18.3 us
    convert_element_type x1, other arithmetic, local(): (split * volume.reshape(block_count, 1, block_size, 1) * norm_factor).ast...  13.7 us
    dot_general x1, local copies, waits for them, and re-layouts, local(): jnp.einsum('bkcr,bkcm->brm', own_blocks, gathered, preferred_element_type...  12.6 us
    scatter-add x1, other arithmetic, local(): applied = applied.at[targets].add(incoming)  9.71 us
    convert_element_type x1, local copies, waits for them, and re-layouts, local(): applied_basis = split.transpose(1, 0, 2, 3).reshape(2, block_count * bloc...  6.61 us
  transfers between devices with their start and end apart: 9, of which 4 were waited for; matrix products, arithmetic and copies ran while one was open for 21% of the time, Pallas kernels for 0%

commit v1 on v0

v1 whole, which is shorter than its diff:
```python
import functools
import math

import jax
import jax.numpy as jnp
from jax import lax
from jax.experimental import pallas as pl
from jax.experimental.pallas import tpu as pltpu
from jax.sharding import PartitionSpec as P

MESH = pl.DeviceIdType.MESH
F32, BF16, I32 = jnp.float32, jnp.bfloat16, jnp.int32

ROWS = 96
KOWN = 7
BS = 64
MODES = 256
NB = 8
SLOTS = 4 * NB
UNROLL = 16
STEPS = ROWS // UNROLL
PROJ = 8

CONTRACT_FIRST = (((0,), (0,)), ((), ()))


def place():
    s = lax.axis_index("stream")
    c = lax.axis_index("cross")
    return (s // 4, s % 4, c // 4, (c // 2) % 2), c % 2


def ident(chip, core):
    return (chip[0] * 4 + chip[1], chip[2] * 4 + chip[3] * 2 + core)


def kernel(
    norm,
    own_cols, border_cols, border_rows,
    basis_h, volume, own_h, border_h,
    applied_out, reduced_out,
    own, basis, sums, volb, send_rows, send_b, recv_rows, recv_a, recv_b, table_v, table,
    w_chunk, w_slot, part, q, pair, h, recv_yz, recv_x,
    own_sem, basis_sem, table_sem, rows_ss, rows_rs, a_ss, a_rs, b_ss, b_rs, pair_sem, yz_sem, x_sem,
):
    s, c = lax.axis_index("stream"), lax.axis_index("cross")
    chip, core = place()
    xl, y, z, xh = chip
    mate = ident(chip, 1 - core)

    def yz_peer(k):
        return (xl, (y + k // 4) % 4, (z + k % 4) % 4, xh)

    def x_peer(k):
        return ((xl + k // 2) % 2, y, z, (xh + k % 2) % 2)

    sides = [
        (s < 7, (s + 1, c), s > 0),
        (s > 0, (s - 1, c), s < 7),
        (c < 15, (s, c + 1), c > 0),
        (c > 0, (s, c - 1), c < 15),
    ]

    basis_copy = pltpu.make_async_copy(basis_h, basis, basis_sem)
    basis_copy.start()

    def own_copy(step):
        rows = pl.ds(step * UNROLL, UNROLL)
        return pltpu.make_async_copy(own_h.at[rows], own.at[rows], own_sem.at[step])

    barrier = pltpu.get_barrier_semaphore()
    for may_send, target, _ in sides:
        @pl.when(may_send)
        def _():
            pl.semaphore_signal(barrier, inc=1, device_id=target, device_id_type=MESH)
    pl.semaphore_signal(barrier, inc=1, device_id=mate, device_id_type=MESH)

    @pl.loop(1, 16)
    def _(k):
        pl.semaphore_signal(barrier, inc=1, device_id=ident(yz_peer(k), core), device_id_type=MESH)

    for k in range(1, 4):
        pl.semaphore_signal(barrier, inc=1, device_id=ident(x_peer(k), core), device_id_type=MESH)

    for step in range(STEPS):
        own_copy(step).start()

    for d in range(4):
        for n in range(NB):
            send_rows[d, pl.ds(n, 1), :] = jnp.full((1, 128), border_rows[d, n], I32)
    for d, (_, _, may_receive) in enumerate(sides):
        @pl.when(jnp.logical_not(may_receive))
        def _():
            recv_rows[d] = jnp.zeros((NB, 128), I32)
            recv_a[d] = jnp.zeros((NB, BS, 2 * BS), BF16)
            recv_b[d] = jnp.zeros((NB, BS, MODES), BF16)

    basis_copy.wait()
    for d in range(4):
        for n in range(NB):
            send_b[d, n] = basis[border_cols[d, n]]

    greeted = sum(jnp.where(may_receive, 1, 0) for _, _, may_receive in sides)
    pl.semaphore_wait(barrier, greeted + 19)

    def border_copy(d, which):
        source, landing, sent, received = (
            (send_rows, recv_rows, rows_ss, rows_rs),
            (border_h, recv_a, a_ss, a_rs),
            (send_b, recv_b, b_ss, b_rs),
        )[which]
        return pltpu.make_async_remote_copy(
            source.at[d], landing.at[d], sent.at[d], received.at[d],
            device_id=sides[d][1], device_id_type=MESH,
        )

    for which in range(3):
        for d in range(4):
            @pl.when(sides[d][0])
            def _():
                border_copy(d, which).start()

    columns = volume[...].T * norm
    for i in range(ROWS // 2):
        volb[2 * i:2 * i + 2] = jnp.broadcast_to(columns[:, i:i + 1], (128, 128)).reshape(2, BS, 128)

    @pl.loop(0, STEPS)
    def _(step):
        own_copy(step).wait()
        for j in range(UNROLL):
            i = step * UNROLL + j
            gathered = jnp.concatenate([basis[own_cols[k, i]] for k in range(KOWN)], axis=0)
            sums[i] = lax.dot_general(
                own[i].reshape(KOWN * BS, 2 * BS), gathered, CONTRACT_FIRST, preferred_element_type=F32
            )

    for d, (may_send, _, may_receive) in enumerate(sides):
        @pl.when(may_receive)
        def _():
            border_copy(d, 0).wait_recv()
    targets = recv_rows[...].reshape(SLOTS, 128)
    slot = lax.broadcasted_iota(I32, (SLOTS, 128), 0)
    lane = lax.broadcasted_iota(I32, (SLOTS, 128), 1)
    target_lane = jnp.sum(jnp.where(slot == lane, targets, 0), axis=0, keepdims=True)
    target_lane = jnp.broadcast_to(target_lane, (SLOTS, 128))
    source = jnp.max(jnp.where(targets == lane, ROWS + slot, lane), axis=0, keepdims=True)
    base = jnp.max(
        jnp.where((targets == target_lane) & (slot < lane), ROWS + slot, target_lane), axis=0, keepdims=True
    )
    last = 1 - jnp.max(
        jnp.where((targets == target_lane) & (slot > lane), 1, 0), axis=0, keepdims=True
    )
    table_v[0:1, :] = source
    table_v[1:2, :] = base
    table_v[2:3, :] = last
    table_v[3:4, :] = target_lane[0:1]
    table_v[4:8, :] = jnp.zeros((4, 128), I32)
    table_copy = pltpu.make_async_copy(table_v, table, table_sem)
    table_copy.start()
    table_copy.wait()

    part[...] = jnp.zeros_like(part)

    def add_product(left, right):
        product = lax.dot_general(left, right, CONTRACT_FIRST, preferred_element_type=F32)
        for lanes in range(4):
            part[lanes] += product[:, lanes * 128:(lanes + 1) * 128]

    @pl.loop(0, ROWS // PROJ)
    def _(step):
        for j in range(PROJ):
            i = step * PROJ + j
            keep = jnp.where(table[0, i] == i, 1.0, 0.0).astype(F32)
            scale = volb[i] * keep
            scale = jnp.concatenate([scale, scale], axis=1)
            row = sums[i]
            w_chunk[j, :, 0:MODES] = (row[0:BS] * scale).astype(BF16)
            w_chunk[j, :, MODES:2 * MODES] = (row[BS:2 * BS] * scale).astype(BF16)
        left = basis[pl.ds(step * PROJ, PROJ)].reshape(PROJ * BS, MODES)
        add_product(left, w_chunk[...].reshape(PROJ * BS, 2 * MODES))

    for d, (_, _, may_receive) in enumerate(sides):
        @pl.when(may_receive)
        def _():
            border_copy(d, 1).wait_recv()
            border_copy(d, 2).wait_recv()

        for n in range(NB):
            m = d * NB + n
            partial = lax.dot_general(recv_a[d, n], recv_b[d, n], CONTRACT_FIRST, preferred_element_type=F32)
            total = sums[table[1, m]] + partial
            sums[ROWS + m] = total
            row = table[3, m]
            scale = volb[row] * table[2, m].astype(F32)
            scale = jnp.concatenate([scale, scale], axis=1)
            w_slot[n, :, 0:MODES] = (total[0:BS] * scale).astype(BF16)
            w_slot[n, :, MODES:2 * MODES] = (total[BS:2 * BS] * scale).astype(BF16)
        left = jnp.concatenate([basis[table[3, d * NB + n]] for n in range(NB)], axis=0)
        add_product(left, w_slot[...].reshape(NB * BS, 2 * MODES))

    for cc in range(2):
        for r in range(2):
            for lanes in range(4):
                for a in range(2):
                    for b in range(2):
                        q[cc, pl.ds((a * 2 + b) * 8 + lanes * 2 + r, 16, stride=32), :] = part[
                            lanes, pl.ds(a * 128 + b * 4 + 2 * cc + r, 16, stride=8), :
                        ]
    pair_copy = pltpu.make_async_remote_copy(
        q.at[1 - core], pair, pair_sem.at[0], pair_sem.at[1], device_id=mate, device_id_type=MESH
    )
    pair_copy.start()
    pair_copy.wait()
    h[...] = (q[core] + pair[...]).reshape(16, 32, 128)

    @pl.loop(1, 16)
    def _(k):
        to = yz_peer(k)
        pltpu.make_async_remote_copy(
            h.at[to[1] * 4 + to[2]], recv_yz.at[k], yz_sem.at[0], yz_sem.at[1],
            device_id=ident(to, core), device_id_type=MESH,
        ).start()

    @pl.loop(0, ROWS // 4)
    def _(step):
        for j in range(4):
            i = step * 4 + j
            row = sums[table[0, i]]
            applied_out[0, i] = row[0:BS].astype(BF16)
            applied_out[1, i] = row[BS:2 * BS].astype(BF16)

    pltpu.make_async_remote_copy(
        h.at[pl.ds(1, 15)], recv_yz.at[pl.ds(1, 15)], yz_sem.at[0], yz_sem.at[1],
        device_id=mate, device_id_type=MESH,
    ).wait()
    recv_yz[0] = h[y * 4 + z]
    h[0] = recv_yz[...].sum(axis=0)
    for k in range(1, 4):
        to = x_peer(k)
        block = pl.ds(pl.multiple_of((to[0] * 2 + to[3]) * 8, 8), 8)
        pltpu.make_async_remote_copy(
            h.at[0, block], recv_x.at[k], x_sem.at[0], x_sem.at[1],
            device_id=ident(to, core), device_id_type=MESH,
        ).start()
    pltpu.make_async_remote_copy(
        recv_x.at[pl.ds(1, 3)], recv_x.at[pl.ds(1, 3)], x_sem.at[0], x_sem.at[1],
        device_id=mate, device_id_type=MESH,
    ).wait()
    recv_x[0] = h[0, pl.ds(pl.multiple_of((xl * 2 + xh) * 8, 8), 8)]
    mine = recv_x[...].sum(axis=0)
    for r in range(2):
        for lanes in range(4):
            reduced_out[r, lanes // 2:lanes // 2 + 1, (lanes % 2) * 128:(lanes % 2 + 1) * 128] = mine[
                lanes * 2 + r:lanes * 2 + r + 1
            ]

    for d, (may_send, _, _) in enumerate(sides):
        @pl.when(may_send)
        def _():
            for which in range(3):
                border_copy(d, which).wait_send()


def local(basis, volume, own_blocks, own_cols, border_blocks, border_cols, border_rows):
    norm = 1.0 / math.sqrt(lax.axis_size("stream") * lax.axis_size("cross") * ROWS * BS)
    smem = pl.BlockSpec(memory_space=pltpu.SMEM)
    vmem = pl.BlockSpec(memory_space=pltpu.VMEM)
    anywhere = pl.BlockSpec(memory_space=pl.ANY)
    dma = pltpu.SemaphoreType.DMA
    applied, reduced = pl.pallas_call(
        functools.partial(kernel, norm),
        name="galerkin",
        in_specs=[smem, smem, smem, anywhere, vmem, anywhere, anywhere],
        out_specs=[vmem, vmem],
        out_shape=[
            jax.ShapeDtypeStruct((2, ROWS, BS, MODES), BF16),
            jax.ShapeDtypeStruct((2, 2, MODES), F32),
        ],
        scratch_shapes=[
            pltpu.VMEM((ROWS, KOWN, BS, 2 * BS), BF16),
            pltpu.VMEM((ROWS, BS, MODES), BF16),
            pltpu.VMEM((ROWS + SLOTS, 2 * BS, MODES), F32),
            pltpu.VMEM((ROWS, BS, 128), F32),
            pltpu.VMEM((4, NB, 128), I32),
            pltpu.VMEM((4, NB, BS, MODES), BF16),
            pltpu.VMEM((4, NB, 128), I32),
            pltpu.VMEM((4, NB, BS, 2 * BS), BF16),
            pltpu.VMEM((4, NB, BS, MODES), BF16),
            pltpu.VMEM((8, 128), I32),
            pltpu.SMEM((8, 128), I32),
            pltpu.VMEM((PROJ, BS, 2 * MODES), BF16),
            pltpu.VMEM((NB, BS, 2 * MODES), BF16),
            pltpu.VMEM((4, MODES, 128), F32),
            pltpu.VMEM((2, 512, 128), F32),
            pltpu.VMEM((512, 128), F32),
            pltpu.VMEM((16, 32, 128), F32),
            pltpu.VMEM((16, 32, 128), F32),
            pltpu.VMEM((4, 8, 128), F32),
            dma((STEPS,)), dma(()), dma(()),
            dma((4,)), dma((4,)), dma((4,)), dma((4,)), dma((4,)), dma((4,)),
            dma((2,)), dma((2,)), dma((2,)),
        ],
        compiler_params=pltpu.CompilerParams(
            collective_id=0, has_side_effects=True, vmem_limit_bytes=60 << 20
        ),
        cost_estimate=pl.CostEstimate(flops=4_700_000_000, bytes_accessed=21_000_000, transcendentals=0),
    )(
        own_cols.T,
        border_cols[0],
        border_rows[0],
        basis.reshape(ROWS, BS, MODES),
        volume.reshape(ROWS // 2, 128),
        own_blocks,
        border_blocks[0],
    )
    applied = applied.reshape(2, ROWS * BS, MODES)
    return applied, reduced


def solution(mesh):
    both = ("stream", "cross")
    return jax.shard_map(
        local,
        mesh=mesh,
        in_specs=(
            P(both, None), P(both), P(both, None, None, None), P(both, None),
            P(both, None, None, None, None), P(both, None, None), P(both, None, None),
        ),
        out_specs=(P(None, both, None), P(both, None, None)),
        check_vma=False,
    )
```

time: 294 us -> 49.9 us (0.17)
  waiting for transfers between devices: 154 us -> 0 us
  local copies, waits for them, and re-layouts: 50.8 us -> 6.49 us
  Pallas kernels: 0 us -> 42.5 us
  other arithmetic: 28.1 us -> 0 us
  matrix products: 23 us -> 0 us
  starting transfers between devices: 21.9 us -> 0 us
  between operations: 14.2 us -> 0.65 us
    unnamed x2 -> x0, waiting for transfers between devices: 147 us -> none
    pallas_call x0 -> x1, Pallas kernels: none -> 42.5 us  [local(): pl.pallas_call(functools.partial(kernel, norm), name='galerkin', in_specs...]
    dot_general x3 -> x0, matrix products: 23 us -> none  [the longest x1 18.3 us: local(): jnp.einsum('bkcr,bkcm->brm', own_blocks, gathered, preferred_element_type...]
    ppermute x8 -> x0, starting transfers between devices: 21.8 us -> none  [passed_along(): lax.ppermute(value, axis, [(source, source + steps) for source in range(l...]
    gather x2 -> x0, local copies, waits for them, and re-layouts: 19.9 us -> none  [the longest x1 18.3 us: local(): gathered = basis_blocks[own_cols]]
    dot_general x2 -> x0, local copies, waits for them, and re-layouts: 14.6 us -> none  [the longest x1 12.6 us: local(): jnp.einsum('bkcr,bkcm->brm', own_blocks, gathered, preferred_element_type...]
    convert_element_type x1 -> x0, other arithmetic: 13.7 us -> none  [local(): (split * volume.reshape(block_count, 1, block_size, 1) * norm_factor).ast...]
    scatter-add x1 -> x0, other arithmetic: 9.71 us -> none  [local(): applied = applied.at[targets].add(incoming)]
  transfers between devices with their start and end apart: 9 -> 0, of which waited for: 4 -> 0; matrix products, arithmetic and copies ran while one was open for 21% -> 0% of each run, Pallas kernels for 0% -> 0%
where the time goes in v1:
time: 49.9 us; the launch traced here: 49.7 us
  Pallas kernels  42.5 us (85%)
  local copies, waits for them, and re-layouts  6.49 us (13%)
  between operations  0.65 us (1%)
    pallas_call x1, Pallas kernels, local(): pl.pallas_call(functools.partial(kernel, norm), name='galerkin', in_specs...  42.5 us
    unnamed x4, local copies, waits for them, and re-layouts  6.49 us

profile of v1, /device:TPU:0, one launch (start us, length us, event | category | flops | bytes accessed | tf_op | source)
XLA Modules:
  0.0 49.7 jit_solution(11593989237402448319)
XLA Ops:
  0.6 42.5 %galerkin.1 = (bf16[2,96,64,256]{3,2,1,0:T(8,128)(2,1)}, f32[2,2,256]{2,1,0:T(2,128)}) custom-call(s32[7,96]{1,0:T(8,128)} %bitcast.11, s32[4,8]{1,0:T(4,128)} %bitcast.12, s32[4,8]{1,0:T(4,128)} %bitcast.13, bf16[96,64,256]{2,1,0:T(8,128)(2,1)} %bitcast.8, f32[48,128]{1,0:T(8,128)} %bitcast.10, bf16[96,7,64,128]{3,2,1,0:T(8,128)(2,1)} %own_h.1, ...), custom_call_target="tpu_custom_call" | custom-call | flops 4700000256 | bytes 21000000 | tf_op jit(solution)/shard_map/galerkin/pallas_call | solution.py:270
  43.2 0.0 copy-start
  43.2 5.9 %copy.11 = bf16[2,6144,256]{2,1,0:T(8,128)(2,1)} copy(bf16[2,6144,256]{2,1,0:T(8,128)(2,1)} %bitcast.7) | data formatting | bytes 12582912
  49.1 0.0 copy-done
  49.1 0.6 %copy.12 = f32[2,2,256]{2,1,0:T(2,128)} copy(f32[2,2,256]{2,1,0:T(2,128)S(1)} %copy-done) | data formatting | bytes 8192
Async XLA Ops:
  43.2 5.9 %copy-start = (f32[2,2,256]{2,1,0:T(2,128)S(1)}, f32[2,2,256]{2,1,0:T(2,128)}, u32[]{:S(2)}) copy-start(f32[2,2,256]{2,1,0:T(2,128)} %get-tuple-element.9) | copy-start | bytes 12292

commit v2 on v1

v2 whole, which is shorter than its diff:
```python
import functools
import math

import jax
import jax.numpy as jnp
from jax import lax
from jax.experimental import pallas as pl
from jax.experimental.pallas import tpu as pltpu
from jax.sharding import PartitionSpec as P

MESH = pl.DeviceIdType.MESH
F32, BF16, I32 = jnp.float32, jnp.bfloat16, jnp.int32

ROWS = 96
KOWN = 7
BS = 64
MODES = 256
NB = 8
SLOTS = 4 * NB
UNROLL = 16
STEPS = ROWS // UNROLL
PROJ = 8

CONTRACT_FIRST = (((0,), (0,)), ((), ()))


def ident(chip, core):
    x, y, z = chip
    return ((x % 2) * 4 + y, z * 4 + (x // 2) * 2 + core)


def moved(chip, dx, dy, dz):
    x, y, z = chip
    return ((x + dx) % 4, (y + dy) % 4, (z + dz) % 4)


AROUND = ((1, 0, 0), (3, 0, 0), (0, 1, 0), (0, 3, 0), (0, 0, 1), (0, 0, 3))
ROUNDS = (AROUND, ((0, 3, 1), (0, 1, 1)), ((0, 3, 2), (2, 0, 0)))
ORDER = (2, 3, 0, 1)
HALF = NB // 2


def kernel(
    norm,
    own_cols, border_cols, border_rows,
    basis_h, volume, own_h, border_h,
    applied_out, reduced_out,
    own, basis, sums, volb, send_rows, send_b, recv_rows, recv_a, recv_b, relay_a, relay_b, table_v, table,
    w_chunk, w_slot, part, q, pair, h, recv_h,
    own_sem, basis_sem, table_sem, rows_ss, rows_rs, a_ss, a_rs, b_ss, b_rs,
    in_ss, in_rs, out_ss, pair_sem, all_sem, known,
):
    s, c = lax.axis_index("stream"), lax.axis_index("cross")
    x, y, z = chip = ((c // 2) % 2 * 2 + s // 4, s % 4, c // 4)
    core = c % 2
    mate = ident(chip, 1 - core)

    def tell(number):
        for step in ROUNDS[number]:
            pl.semaphore_signal(known.at[number], inc=1, device_id=ident(moved(chip, *step), core), device_id_type=MESH)

    def told(number):
        pl.semaphore_wait(known.at[number], len(ROUNDS[number]))

    sides = [
        (c < 15, (s, c + 1), c > 0),
        (c > 0, (s, c - 1), c < 15),
        (s < 7, (s + 1, c), s > 0),
        (s > 0, (s - 1, c), s < 7),
    ]
    corners = ((2, 3, 0, 4), (3, 4, 7, 3))

    basis_copy = pltpu.make_async_copy(basis_h, basis, basis_sem)
    basis_copy.start()

    def own_copy(step):
        rows = pl.ds(step * UNROLL, UNROLL)
        return pltpu.make_async_copy(own_h.at[rows], own.at[rows], own_sem.at[step])

    barrier = pltpu.get_barrier_semaphore()
    for may_send, target, _ in sides:
        @pl.when(may_send)
        def _():
            pl.semaphore_signal(barrier, inc=1, device_id=target, device_id_type=MESH)
    pl.semaphore_signal(barrier, inc=1, device_id=mate, device_id_type=MESH)

    for step in AROUND:
        pl.semaphore_signal(barrier, inc=1, device_id=ident(moved(chip, *step), core), device_id_type=MESH)

    for step in range(STEPS):
        own_copy(step).start()

    for d in range(4):
        for n in range(NB):
            send_rows[d, pl.ds(n, 1), :] = jnp.full((1, 128), border_rows[ORDER[d], n], I32)
    for d, (_, _, may_receive) in enumerate(sides):
        @pl.when(jnp.logical_not(may_receive))
        def _():
            recv_rows[d] = jnp.zeros((NB, 128), I32)
            recv_a[d] = jnp.zeros((NB, BS, 2 * BS), BF16)
            recv_b[d] = jnp.zeros((NB, BS, MODES), BF16)

    basis_copy.wait()
    for d in range(4):
        for n in range(NB):
            send_b[d, n] = basis[border_cols[ORDER[d], n]]

    greeted = sum(jnp.where(may_receive, 1, 0) for _, _, may_receive in sides)
    pl.semaphore_wait(barrier, greeted + 1 + len(AROUND))

    tell(0)

    def rows_copy(d):
        return pltpu.make_async_remote_copy(
            send_rows.at[d], recv_rows.at[d], rows_ss.at[d], rows_rs.at[d], device_id=sides[d][1], device_id_type=MESH
        )

    def half_copies(d, half):
        blocks = pl.ds(half * HALF, HALF)
        return (
            pltpu.make_async_remote_copy(
                border_h.at[ORDER[d], blocks], recv_a.at[d, blocks], a_ss.at[d, half], a_rs.at[d, half],
                device_id=sides[d][1], device_id_type=MESH,
            ),
            pltpu.make_async_remote_copy(
                send_b.at[d, blocks], recv_b.at[d, blocks], b_ss.at[d, half], b_rs.at[d, half],
                device_id=sides[d][1], device_id_type=MESH,
            ),
        )

    def corner_copies(d, corner, k):
        return (
            pltpu.make_async_remote_copy(
                border_h.at[ORDER[d], HALF + k], relay_a.at[k], in_ss.at[0, k], in_rs.at[0, k],
                device_id=(corner, c), device_id_type=MESH,
            ),
            pltpu.make_async_remote_copy(
                send_b.at[d, HALF + k], relay_b.at[k], in_ss.at[1, k], in_rs.at[1, k],
                device_id=(corner, c), device_id_type=MESH,
            ),
        )

    def onward_copies(d, receiver, k):
        return (
            pltpu.make_async_remote_copy(
                relay_a.at[k], recv_a.at[d, HALF + k], out_ss.at[0, k], a_rs.at[d, 1],
                device_id=(receiver, c), device_id_type=MESH,
            ),
            pltpu.make_async_remote_copy(
                relay_b.at[k], recv_b.at[d, HALF + k], out_ss.at[1, k], b_rs.at[d, 1],
                device_id=(receiver, c), device_id_type=MESH,
            ),
        )

    for d in range(4):
        @pl.when(sides[d][0])
        def _():
            rows_copy(d).start()
    by_corner = {d: (sender, corner) for d, sender, corner, _ in corners}
    for d, (sender, corner) in by_corner.items():
        @pl.when(s == sender)
        def _():
            for k in range(HALF):
                for copy in corner_copies(d, corner, k):
                    copy.start()
    for half in (0, 1):
        for d in (2, 3, 0, 1):
            direct = sides[d][0]
            if half and d in by_corner:
                direct = jnp.logical_and(direct, s != by_corner[d][0])

            @pl.when(direct)
            def _():
                for copy in half_copies(d, half):
                    copy.start()

    columns = volume[...].T * norm
    for i in range(ROWS // 2):
        volb[2 * i:2 * i + 2] = jnp.broadcast_to(columns[:, i:i + 1], (128, 128)).reshape(2, BS, 128)

    @pl.loop(0, STEPS)
    def _(step):
        own_copy(step).wait()
        for d, _, corner, receiver in corners:
            @pl.when(jnp.logical_and(step >= STEPS - HALF, s == corner))
            def _():
                k = step - (STEPS - HALF)
                for copy in corner_copies(d, corner, k):
                    copy.wait_recv()
                for copy in onward_copies(d, receiver, k):
                    copy.start()

        @pl.when(step == 2)
        def _():
            told(0)
            tell(1)

        @pl.when(step == 4)
        def _():
            told(1)
            tell(2)

        for j in range(UNROLL):
            i = step * UNROLL + j
            gathered = jnp.concatenate([basis[own_cols[k, i]] for k in range(KOWN)], axis=0)
            sums[i] = lax.dot_general(
                own[i].reshape(KOWN * BS, 2 * BS), gathered, CONTRACT_FIRST, preferred_element_type=F32
            )

    for d, (may_send, _, may_receive) in enumerate(sides):
        @pl.when(may_receive)
        def _():
            rows_copy(d).wait_recv()
    targets = recv_rows[...].reshape(SLOTS, 128)
    slot = lax.broadcasted_iota(I32, (SLOTS, 128), 0)
    lane = lax.broadcasted_iota(I32, (SLOTS, 128), 1)
    target_lane = jnp.sum(jnp.where(slot == lane, targets, 0), axis=0, keepdims=True)
    target_lane = jnp.broadcast_to(target_lane, (SLOTS, 128))
    source = jnp.max(jnp.where(targets == lane, ROWS + slot, lane), axis=0, keepdims=True)
    base = jnp.max(
        jnp.where((targets == target_lane) & (slot < lane), ROWS + slot, target_lane), axis=0, keepdims=True
    )
    last = 1 - jnp.max(
        jnp.where((targets == target_lane) & (slot > lane), 1, 0), axis=0, keepdims=True
    )
    table_v[0:1, :] = source
    table_v[1:2, :] = base
    table_v[2:3, :] = last
    table_v[3:4, :] = target_lane[0:1]
    table_v[4:8, :] = jnp.zeros((4, 128), I32)
    table_copy = pltpu.make_async_copy(table_v, table, table_sem)
    table_copy.start()
    table_copy.wait()

    part[...] = jnp.zeros_like(part)

    def add_product(left, right):
        product = lax.dot_general(left, right, CONTRACT_FIRST, preferred_element_type=F32)
        for lanes in range(4):
            part[lanes] += product[:, lanes * 128:(lanes + 1) * 128]

    @pl.loop(0, ROWS // PROJ)
    def _(step):
        for j in range(PROJ):
            i = step * PROJ + j
            keep = jnp.where(table[0, i] == i, 1.0, 0.0).astype(F32)
            scale = volb[i] * keep
            scale = jnp.concatenate([scale, scale], axis=1)
            row = sums[i]
            w_chunk[j, :, 0:MODES] = (row[0:BS] * scale).astype(BF16)
            w_chunk[j, :, MODES:2 * MODES] = (row[BS:2 * BS] * scale).astype(BF16)
        left = basis[pl.ds(step * PROJ, PROJ)].reshape(PROJ * BS, MODES)
        add_product(left, w_chunk[...].reshape(PROJ * BS, 2 * MODES))

    for part_at in range(8):
        d, half = part_at // 2, part_at % 2

        @pl.when(sides[d][2])
        def _():
            for copy in half_copies(d, half):
                copy.wait_recv()

        first = d * NB + half * HALF
        for j in range(HALF):
            n = half * HALF + j
            m = first + j
            partial = lax.dot_general(recv_a[d, n], recv_b[d, n], CONTRACT_FIRST, preferred_element_type=F32)
            total = sums[table[1, m]] + partial
            sums[ROWS + m] = total
            row = table[3, m]
            scale = volb[row] * table[2, m].astype(F32)
            scale = jnp.concatenate([scale, scale], axis=1)
            w_slot[j, :, 0:MODES] = (total[0:BS] * scale).astype(BF16)
            w_slot[j, :, MODES:2 * MODES] = (total[BS:2 * BS] * scale).astype(BF16)
        left = jnp.concatenate([basis[table[3, first + j]] for j in range(HALF)], axis=0)
        add_product(left, w_slot[...].reshape(HALF * BS, 2 * MODES))

    told(2)

    for cc in range(2):
        for r in range(2):
            for lanes in range(4):
                for at in range(4):
                    q[cc, pl.ds(at * 128 + lanes * 2 + r, 16, stride=8), :] = part[
                        lanes, pl.ds((at % 2) * 128 + (at // 2) * 4 + 2 * cc + r, 16, stride=8), :
                    ]
    pair_copy = pltpu.make_async_remote_copy(
        q.at[1 - core], pair, pair_sem.at[0], pair_sem.at[1], device_id=mate, device_id_type=MESH
    )
    pair_copy.start()
    pair_copy.wait()
    h[...] = (q[core] + pair[...]).reshape(64, 8, 128)

    @pl.loop(1, 64)
    def _(k):
        to = moved(chip, k // 16, (k // 4) % 4, k % 4)
        pltpu.make_async_remote_copy(
            h.at[to[0] * 16 + to[1] * 4 + to[2]], recv_h.at[k], all_sem.at[0], all_sem.at[1],
            device_id=ident(to, core), device_id_type=MESH,
        ).start()

    @pl.loop(0, ROWS // 4)
    def _(step):
        for j in range(4):
            i = step * 4 + j
            row = sums[table[0, i]]
            applied_out[0, i] = row[0:BS].astype(BF16)
            applied_out[1, i] = row[BS:2 * BS].astype(BF16)

    pltpu.make_async_remote_copy(
        h.at[pl.ds(1, 63)], recv_h.at[pl.ds(1, 63)], all_sem.at[0], all_sem.at[1], device_id=mate, device_id_type=MESH
    ).wait()
    recv_h[0] = h[x * 16 + y * 4 + z]
    mine = recv_h[...].sum(axis=0)
    for r in range(2):
        for lanes in range(4):
            reduced_out[r, lanes // 2:lanes // 2 + 1, (lanes % 2) * 128:(lanes % 2 + 1) * 128] = mine[
                lanes * 2 + r:lanes * 2 + r + 1
            ]

    for d, (may_send, _, _) in enumerate(sides):
        @pl.when(may_send)
        def _():
            rows_copy(d).wait_send()
            for copy in half_copies(d, 0):
                copy.wait_send()

        direct = may_send
        if d in by_corner:
            direct = jnp.logical_and(may_send, s != by_corner[d][0])

        @pl.when(direct)
        def _():
            for copy in half_copies(d, 1):
                copy.wait_send()
    for d, sender, corner, receiver in corners:
        @pl.when(s == sender)
        def _():
            for k in range(HALF):
                for copy in corner_copies(d, corner, k):
                    copy.wait_send()

        @pl.when(s == corner)
        def _():
            for k in range(HALF):
                for copy in onward_copies(d, receiver, k):
                    copy.wait_send()


def local(basis, volume, own_blocks, own_cols, border_blocks, border_cols, border_rows):
    norm = 1.0 / math.sqrt(lax.axis_size("stream") * lax.axis_size("cross") * ROWS * BS)
    smem = pl.BlockSpec(memory_space=pltpu.SMEM)
    vmem = pl.BlockSpec(memory_space=pltpu.VMEM)
    anywhere = pl.BlockSpec(memory_space=pl.ANY)
    dma = pltpu.SemaphoreType.DMA
    applied, reduced = pl.pallas_call(
        functools.partial(kernel, norm),
        name="galerkin",
        in_specs=[smem, smem, smem, anywhere, vmem, anywhere, anywhere],
        out_specs=[vmem, vmem],
        out_shape=[
            pltpu.VMEM((2, ROWS, BS, MODES), BF16),
            pltpu.VMEM((2, 2, MODES), F32),
        ],
        scratch_shapes=[
            pltpu.VMEM((ROWS, KOWN, BS, 2 * BS), BF16),
            pltpu.VMEM((ROWS, BS, MODES), BF16),
            pltpu.VMEM((ROWS + SLOTS, 2 * BS, MODES), F32),
            pltpu.VMEM((ROWS, BS, 128), F32),
            pltpu.VMEM((4, NB, 128), I32),
            pltpu.VMEM((4, NB, BS, MODES), BF16),
            pltpu.VMEM((4, NB, 128), I32),
            pltpu.VMEM((4, NB, BS, 2 * BS), BF16),
            pltpu.VMEM((4, NB, BS, MODES), BF16),
            pltpu.VMEM((HALF, BS, 2 * BS), BF16),
            pltpu.VMEM((HALF, BS, MODES), BF16),
            pltpu.VMEM((8, 128), I32),
            pltpu.SMEM((8, 128), I32),
            pltpu.VMEM((PROJ, BS, 2 * MODES), BF16),
            pltpu.VMEM((HALF, BS, 2 * MODES), BF16),
            pltpu.VMEM((4, MODES, 128), F32),
            pltpu.VMEM((2, 512, 128), F32),
            pltpu.VMEM((512, 128), F32),
            pltpu.VMEM((64, 8, 128), F32),
            pltpu.VMEM((64, 8, 128), F32),
            dma((STEPS,)), dma(()), dma(()),
            dma((4,)), dma((4,)), dma((4, 2)), dma((4, 2)), dma((4, 2)), dma((4, 2)),
            dma((2, HALF)), dma((2, HALF)), dma((2, HALF)),
            dma((2,)), dma((2,)), pltpu.SemaphoreType.REGULAR((len(ROUNDS),)),
        ],
        compiler_params=pltpu.CompilerParams(
            collective_id=0, has_side_effects=True, vmem_limit_bytes=48 << 20
        ),
        cost_estimate=pl.CostEstimate(flops=4_700_000_000, bytes_accessed=21_000_000, transcendentals=0),
    )(
        own_cols.T,
        border_cols[0],
        border_rows[0],
        basis.reshape(ROWS, BS, MODES),
        volume.reshape(ROWS // 2, 128),
        own_blocks,
        border_blocks[0],
    )
    applied = applied.reshape(2, ROWS * BS, MODES)
    return applied, reduced


def solution(mesh):
    both = ("stream", "cross")
    return jax.shard_map(
        local,
        mesh=mesh,
        in_specs=(
            P(both, None), P(both), P(both, None, None, None), P(both, None),
            P(both, None, None, None, None), P(both, None, None), P(both, None, None),
        ),
        out_specs=(P(None, both, None), P(both, None, None)),
        check_vma=False,
    )
```

time: 49.9 us -> 40.3 us (0.81)
  Pallas kernels: 42.5 us -> 36.2 us
  local copies, waits for them, and re-layouts: 6.49 us -> 3.3 us
    pallas_call x1, Pallas kernels: 42.5 us -> 36.2 us  [local(): pl.pallas_call(functools.partial(kernel, norm), name='galerkin', in_specs...]
    unnamed x4 -> x2, local copies, waits for them, and re-layouts: 6.49 us -> 3.3 us
where the time goes in v2:
time: 40.3 us; the launch traced here: 40.1 us
  Pallas kernels  36.2 us (90%)
  local copies, waits for them, and re-layouts  3.3 us (8%)
  between operations  0.64 us (2%)
    pallas_call x1, Pallas kernels, local(): pl.pallas_call(functools.partial(kernel, norm), name='galerkin', in_specs...  36.2 us
    unnamed x2, local copies, waits for them, and re-layouts  3.3 us

profile of v2, /device:TPU:0, one launch (start us, length us, event | category | flops | bytes accessed | tf_op | source)
XLA Modules:
  0.0 40.1 jit_solution(17350490310155840443)
XLA Ops:
  0.6 36.2 %galerkin.1 = (bf16[2,96,64,256]{3,2,1,0:T(8,128)(2,1)S(1)}, f32[2,2,256]{2,1,0:T(2,128)S(1)}) custom-call(s32[7,96]{1,0:T(8,128)} %bitcast.11, s32[4,8]{1,0:T(4,128)} %bitcast.12, s32[4,8]{1,0:T(4,128)} %bitcast.13, bf16[96,64,256]{2,1,0:T(8,128)(2,1)} %bitcast.8, f32[48,128]{1,0:T(8,128)} %bitcast.10, bf16[96,7,64,128]{3,2,1,0:T(8,128)(2,1)} %own_h.1, ...), custom_call_target="tpu_custom_call" | custom-call | flops 4700000256 | bytes 21000000 | tf_op jit(solution)/shard_map/galerkin/pallas_call | solution.py:356
  36.8 2.7 %copy.11 = bf16[2,6144,256]{2,1,0:T(8,128)(2,1)} copy(bf16[2,6144,256]{2,1,0:T(8,128)(2,1)S(1)} %bitcast.7) | data formatting | bytes 12582912
  39.5 0.6 %copy.12 = f32[2,2,256]{2,1,0:T(2,128)} copy(f32[2,2,256]{2,1,0:T(2,128)S(1)} %get-tuple-element.7) | data formatting | bytes 8192

commit v3 on v2

--- a/solution.py
+++ b/solution.py
@@ -42,13 +42,13 @@
 
 def kernel(
     norm,
-    own_cols, border_cols, border_rows,
-    basis_h, volume, own_h, border_h,
+    own_cols_h, border_cols_h, border_rows_h, basis_h, volume_h, own_h, border_h,
     applied_out, reduced_out,
+    own_cols, border_cols, border_rows, volume,
     own, basis, sums, volb, send_rows, send_b, recv_rows, recv_a, recv_b, relay_a, relay_b, table_v, table,
     w_chunk, w_slot, part, q, pair, h, recv_h,
-    own_sem, basis_sem, table_sem, rows_ss, rows_rs, a_ss, a_rs, b_ss, b_rs,
-    in_ss, in_rs, out_ss, pair_sem, all_sem, known,
+    own_sem, basis_sem, small_sem, table_sem, rows_ss, rows_rs, a_ss, a_rs, b_ss, b_rs,
+    in_ss, in_rs, out_ss, pair_ss, pair_rs, all_sem, known,
 ):
     s, c = lax.axis_index("stream"), lax.axis_index("cross")
     x, y, z = chip = ((c // 2) % 2 * 2 + s // 4, s % 4, c // 4)
@@ -68,8 +68,17 @@
         (s < 7, (s + 1, c), s > 0),
         (s > 0, (s - 1, c), s < 7),
     ]
+    lands = (0, 1, jnp.where(s == 3, 3, 2), jnp.where(s == 5, 2, 3))
     corners = ((2, 3, 0, 4), (3, 4, 7, 3))
 
+    small_copies = [
+        pltpu.make_async_copy(source, landing, small_sem.at[i])
+        for i, (source, landing) in enumerate((
+            (border_cols_h, border_cols), (border_rows_h, border_rows), (own_cols_h, own_cols), (volume_h, volume),
+        ))
+    ]
+    small_copies[0].start()
+    small_copies[1].start()
     basis_copy = pltpu.make_async_copy(basis_h, basis, basis_sem)
     basis_copy.start()
 
@@ -87,92 +96,108 @@
     for step in AROUND:
         pl.semaphore_signal(barrier, inc=1, device_id=ident(moved(chip, *step), core), device_id_type=MESH)
 
-    for step in range(STEPS):
-        own_copy(step).start()
-
+    for copy in small_copies[2:]:
+        copy.start()
+
+    for d, (_, _, may_receive) in enumerate(sides):
+        @pl.when(jnp.logical_not(may_receive))
+        def _():
+            recv_rows[d] = jnp.zeros((NB, 128), I32)
+            recv_a[d] = jnp.zeros((NB, BS, 2 * BS), BF16)
+            recv_b[d] = jnp.zeros((NB, BS, MODES), BF16)
+
+    small_copies[1].wait()
     for d in range(4):
         for n in range(NB):
             send_rows[d, pl.ds(n, 1), :] = jnp.full((1, 128), border_rows[ORDER[d], n], I32)
-    for d, (_, _, may_receive) in enumerate(sides):
-        @pl.when(jnp.logical_not(may_receive))
-        def _():
-            recv_rows[d] = jnp.zeros((NB, 128), I32)
-            recv_a[d] = jnp.zeros((NB, BS, 2 * BS), BF16)
-            recv_b[d] = jnp.zeros((NB, BS, MODES), BF16)
-
+    greeted = sum(jnp.where(may_receive, 1, 0) for _, _, may_receive in sides)
+    pl.semaphore_wait(barrier, greeted + 1 + len(AROUND))
+
+    def rows_copy(d, land):
+        return pltpu.make_async_remote_copy(
+            send_rows.at[d], recv_rows.at[land], rows_ss.at[d], rows_rs.at[land],
+            device_id=sides[d][1], device_id_type=MESH,
+        )
+
+    def half_copies(d, half, land):
+        blocks = pl.ds(half * HALF, HALF)
+        return (
+            pltpu.make_async_remote_copy(
+                border_h.at[ORDER[d], blocks], recv_a.at[land, blocks], a_ss.at[d, half], a_rs.at[land, half],
+                device_id=sides[d][1], device_id_type=MESH,
+            ),
+            pltpu.make_async_remote_copy(
+                send_b.at[d, blocks], recv_b.at[land, blocks], b_ss.at[d, half], b_rs.at[land, half],
+                device_id=sides[d][1], device_id_type=MESH,
+            ),
+        )
+
+    def corner_copies(d, corner, k):
+        return (
+            pltpu.make_async_remote_copy(
+                border_h.at[ORDER[d], HALF + k], relay_a.at[k], in_ss.at[0, k], in_rs.at[0, k],
+                device_id=(corner, c), device_id_type=MESH,
+            ),
+            pltpu.make_async_remote_copy(
+                send_b.at[d, HALF + k], relay_b.at[k], in_ss.at[1, k], in_rs.at[1, k],
+                device_id=(corner, c), device_id_type=MESH,
+            ),
+        )
+
+    def onward_copies(receiver, k):
+        return (
+            pltpu.make_async_remote_copy(
+                relay_a.at[k], recv_a.at[3, HALF + k], out_ss.at[0, k], a_rs.at[3, 1],
+                device_id=(receiver, c), device_id_type=MESH,
+            ),
+            pltpu.make_async_remote_copy(
+                relay_b.at[k], recv_b.at[3, HALF + k], out_ss.at[1, k], b_rs.at[3, 1],
+                device_id=(receiver, c), device_id_type=MESH,
+            ),
+        )
+
+    by_corner = {d: (sender, corner) for d, sender, corner, _ in corners}
+
+    def send(d, which):
+        @pl.when(sides[d][0])
+        def _():
+            half_copies(d, 0, lands[d])[which].start()
+
+        if d not in by_corner:
+            @pl.when(sides[d][0])
+            def _():
+                half_copies(d, 1, lands[d])[which].start()
+
+            return
+        sender, corner = by_corner[d]
+
+        @pl.when(s == sender)
+        def _():
+            for k in range(HALF):
+                corner_copies(d, corner, k)[which].start()
+
+        @pl.when(jnp.logical_and(sides[d][0], s != sender))
+        def _():
+            half_copies(d, 1, lands[d])[which].start()
+
+    for d in range(4):
+        @pl.when(sides[d][0])
+        def _():
+            rows_copy(d, lands[d]).start()
+
+    for d in (2, 3, 0, 1):
+        send(d, 0)
+    small_copies[0].wait()
     basis_copy.wait()
-    for d in range(4):
+    for d in (2, 3, 0, 1):
         for n in range(NB):
             send_b[d, n] = basis[border_cols[ORDER[d], n]]
-
-    greeted = sum(jnp.where(may_receive, 1, 0) for _, _, may_receive in sides)
-    pl.semaphore_wait(barrier, greeted + 1 + len(AROUND))
-
+        send(d, 1)
+    for step in range(STEPS):
+        own_copy(step).start()
     tell(0)
-
-    def rows_copy(d):
-        return pltpu.make_async_remote_copy(
-            send_rows.at[d], recv_rows.at[d], rows_ss.at[d], rows_rs.at[d], device_id=sides[d][1], device_id_type=MESH
-        )
-
-    def half_copies(d, half):
-        blocks = pl.ds(half * HALF, HALF)
-        return (
-            pltpu.make_async_remote_copy(
-                border_h.at[ORDER[d], blocks], recv_a.at[d, blocks], a_ss.at[d, half], a_rs.at[d, half],
-                device_id=sides[d][1], device_id_type=MESH,
-            ),
-            pltpu.make_async_remote_copy(
-                send_b.at[d, blocks], recv_b.at[d, blocks], b_ss.at[d, half], b_rs.at[d, half],
-                device_id=sides[d][1], device_id_type=MESH,
-            ),
-        )
-
-    def corner_copies(d, corner, k):
-        return (
-            pltpu.make_async_remote_copy(
-                border_h.at[ORDER[d], HALF + k], relay_a.at[k], in_ss.at[0, k], in_rs.at[0, k],
-                device_id=(corner, c), device_id_type=MESH,
-            ),
-            pltpu.make_async_remote_copy(
-                send_b.at[d, HALF + k], relay_b.at[k], in_ss.at[1, k], in_rs.at[1, k],
-                device_id=(corner, c), device_id_type=MESH,
-            ),
-        )
-
-    def onward_copies(d, receiver, k):
-        return (
-            pltpu.make_async_remote_copy(
-                relay_a.at[k], recv_a.at[d, HALF + k], out_ss.at[0, k], a_rs.at[d, 1],
-                device_id=(receiver, c), device_id_type=MESH,
-            ),
-            pltpu.make_async_remote_copy(
-                relay_b.at[k], recv_b.at[d, HALF + k], out_ss.at[1, k], b_rs.at[d, 1],
-                device_id=(receiver, c), device_id_type=MESH,
-            ),
-        )
-
-    for d in range(4):
-        @pl.when(sides[d][0])
-        def _():
-            rows_copy(d).start()
-    by_corner = {d: (sender, corner) for d, sender, corner, _ in corners}
-    for d, (sender, corner) in by_corner.items():
-        @pl.when(s == sender)
-        def _():
-            for k in range(HALF):
-                for copy in corner_copies(d, corner, k):
-                    copy.start()
-    for half in (0, 1):
-        for d in (2, 3, 0, 1):
-            direct = sides[d][0]
-            if half and d in by_corner:
-                direct = jnp.logical_and(direct, s != by_corner[d][0])
-
-            @pl.when(direct)
-            def _():
-                for copy in half_copies(d, half):
-                    copy.start()
+    small_copies[2].wait()
+    small_copies[3].wait()
 
     columns = volume[...].T * norm
     for i in range(ROWS // 2):
@@ -187,7 +212,7 @@
                 k = step - (STEPS - HALF)
                 for copy in corner_copies(d, corner, k):
                     copy.wait_recv()
-                for copy in onward_copies(d, receiver, k):
+                for copy in onward_copies(receiver, k):
                     copy.start()
 
         @pl.when(step == 2)
@@ -210,7 +235,7 @@
     for d, (may_send, _, may_receive) in enumerate(sides):
         @pl.when(may_receive)
         def _():
-            rows_copy(d).wait_recv()
+            rows_copy(d, d).wait_recv()
     targets = recv_rows[...].reshape(SLOTS, 128)
     slot = lax.broadcasted_iota(I32, (SLOTS, 128), 0)
     lane = lax.broadcasted_iota(I32, (SLOTS, 128), 1)
@@ -252,28 +277,25 @@
         left = basis[pl.ds(step * PROJ, PROJ)].reshape(PROJ * BS, MODES)
         add_product(left, w_chunk[...].reshape(PROJ * BS, 2 * MODES))
 
-    for part_at in range(8):
-        d, half = part_at // 2, part_at % 2
-
+    for d in range(4):
         @pl.when(sides[d][2])
         def _():
-            for copy in half_copies(d, half):
-                copy.wait_recv()
-
-        first = d * NB + half * HALF
-        for j in range(HALF):
-            n = half * HALF + j
-            m = first + j
+            for half in range(2):
+                for copy in half_copies(d, half, d):
+                    copy.wait_recv()
+
+        for n in range(NB):
+            m = d * NB + n
             partial = lax.dot_general(recv_a[d, n], recv_b[d, n], CONTRACT_FIRST, preferred_element_type=F32)
             total = sums[table[1, m]] + partial
             sums[ROWS + m] = total
             row = table[3, m]
             scale = volb[row] * table[2, m].astype(F32)
             scale = jnp.concatenate([scale, scale], axis=1)
-            w_slot[j, :, 0:MODES] = (total[0:BS] * scale).astype(BF16)
-            w_slot[j, :, MODES:2 * MODES] = (total[BS:2 * BS] * scale).astype(BF16)
-        left = jnp.concatenate([basis[table[3, first + j]] for j in range(HALF)], axis=0)
-        add_product(left, w_slot[...].reshape(HALF * BS, 2 * MODES))
+            w_slot[n, :, 0:MODES] = (total[0:BS] * scale).astype(BF16)
+            w_slot[n, :, MODES:2 * MODES] = (total[BS:2 * BS] * scale).astype(BF16)
+        left = jnp.concatenate([basis[table[3, d * NB + n]] for n in range(NB)], axis=0)
+        add_product(left, w_slot[...].reshape(NB * BS, 2 * MODES))
 
     told(2)
 
@@ -284,20 +306,35 @@
                     q[cc, pl.ds(at * 128 + lanes * 2 + r, 16, stride=8), :] = part[
                         lanes, pl.ds((at % 2) * 128 + (at // 2) * 4 + 2 * cc + r, 16, stride=8), :
                     ]
-    pair_copy = pltpu.make_async_remote_copy(
-        q.at[1 - core], pair, pair_sem.at[0], pair_sem.at[1], device_id=mate, device_id_type=MESH
-    )
-    pair_copy.start()
-    pair_copy.wait()
-    h[...] = (q[core] + pair[...]).reshape(64, 8, 128)
-
-    @pl.loop(1, 64)
-    def _(k):
-        to = moved(chip, k // 16, (k // 4) % 4, k % 4)
-        pltpu.make_async_remote_copy(
-            h.at[to[0] * 16 + to[1] * 4 + to[2]], recv_h.at[k], all_sem.at[0], all_sem.at[1],
-            device_id=ident(to, core), device_id_type=MESH,
-        ).start()
+    order = [(x + i) % 4 for i in (2, 1, 3, 0)]
+
+    def pair_copy(i):
+        tiles = pl.ds(pl.multiple_of(order[i] * 128, 128), 128)
+        return pltpu.make_async_remote_copy(
+            q.at[1 - core, tiles], pair.at[tiles], pair_ss.at[i], pair_rs.at[i], device_id=mate, device_id_type=MESH
+        )
+
+    def sum_copy(i, j):
+        from_it = (x - order[i] + 4) % 4 * 16 + (y - j // 4 + 4) % 4 * 4 + (z - j % 4 + 4) % 4
+        return from_it, pltpu.make_async_remote_copy(
+            h.at[order[i] * 16 + j], recv_h.at[from_it], all_sem.at[0], all_sem.at[1],
+            device_id=ident((order[i], j // 4, j % 4), core), device_id_type=MESH,
+        )
+
+    for i in range(4):
+        pair_copy(i).start()
+    for i in range(4):
+        pair_copy(i).wait()
+        tiles = pl.ds(pl.multiple_of(order[i] * 128, 128), 128)
+        h[pl.ds(order[i] * 16, 16)] = (q[core, tiles] + pair[tiles]).reshape(16, 8, 128)
+
+        @pl.loop(0, 16)
+        def _(j):
+            from_it, copy = sum_copy(i, j)
+
+            @pl.when(from_it != 0)
+            def _():
+                copy.start()
 
     @pl.loop(0, ROWS // 4)
     def _(step):
@@ -321,8 +358,8 @@
     for d, (may_send, _, _) in enumerate(sides):
         @pl.when(may_send)
         def _():
-            rows_copy(d).wait_send()
-            for copy in half_copies(d, 0):
+            rows_copy(d, d).wait_send()
+            for copy in half_copies(d, 0, d):
                 copy.wait_send()
 
         direct = may_send
@@ -331,7 +368,7 @@
 
         @pl.when(direct)
         def _():
-            for copy in half_copies(d, 1):
+            for copy in half_copies(d, 1, d):
                 copy.wait_send()
     for d, sender, corner, receiver in corners:
         @pl.when(s == sender)
@@ -343,26 +380,29 @@
         @pl.when(s == corner)
         def _():
             for k in range(HALF):
-                for copy in onward_copies(d, receiver, k):
+                for copy in onward_copies(receiver, k):
                     copy.wait_send()
 
 
 def local(basis, volume, own_blocks, own_cols, border_blocks, border_cols, border_rows):
     norm = 1.0 / math.sqrt(lax.axis_size("stream") * lax.axis_size("cross") * ROWS * BS)
-    smem = pl.BlockSpec(memory_space=pltpu.SMEM)
     vmem = pl.BlockSpec(memory_space=pltpu.VMEM)
     anywhere = pl.BlockSpec(memory_space=pl.ANY)
     dma = pltpu.SemaphoreType.DMA
     applied, reduced = pl.pallas_call(
         functools.partial(kernel, norm),
         name="galerkin",
-        in_specs=[smem, smem, smem, anywhere, vmem, anywhere, anywhere],
+        in_specs=[anywhere] * 7,
         out_specs=[vmem, vmem],
         out_shape=[
             pltpu.VMEM((2, ROWS, BS, MODES), BF16),
             pltpu.VMEM((2, 2, MODES), F32),
         ],
         scratch_shapes=[
+            pltpu.SMEM((KOWN, ROWS), I32),
+            pltpu.SMEM((4, NB), I32),
+            pltpu.SMEM((4, NB), I32),
+            pltpu.VMEM((ROWS // 2, 128), F32),
             pltpu.VMEM((ROWS, KOWN, BS, 2 * BS), BF16),
             pltpu.VMEM((ROWS, BS, MODES), BF16),
             pltpu.VMEM((ROWS + SLOTS, 2 * BS, MODES), F32),
@@ -377,16 +417,16 @@
             pltpu.VMEM((8, 128), I32),
             pltpu.SMEM((8, 128), I32),
             pltpu.VMEM((PROJ, BS, 2 * MODES), BF16),
-            pltpu.VMEM((HALF, BS, 2 * MODES), BF16),
+            pltpu.VMEM((NB, BS, 2 * MODES), BF16),
             pltpu.VMEM((4, MODES, 128), F32),
             pltpu.VMEM((2, 512, 128), F32),
             pltpu.VMEM((512, 128), F32),
             pltpu.VMEM((64, 8, 128), F32),
             pltpu.VMEM((64, 8, 128), F32),
-            dma((STEPS,)), dma(()), dma(()),
+            dma((STEPS,)), dma(()), dma((4,)), dma(()),
             dma((4,)), dma((4,)), dma((4, 2)), dma((4, 2)), dma((4, 2)), dma((4, 2)),
             dma((2, HALF)), dma((2, HALF)), dma((2, HALF)),
-            dma((2,)), dma((2,)), pltpu.SemaphoreType.REGULAR((len(ROUNDS),)),
+            dma((4,)), dma((4,)), dma((2,)), pltpu.SemaphoreType.REGULAR((len(ROUNDS),)),
         ],
         compiler_params=pltpu.CompilerParams(
             collective_id=0, has_side_effects=True, vmem_limit_bytes=48 << 20

time: 40.3 us -> 36.5 us (0.906)
  Pallas kernels: 36.2 us -> 32.3 us
    pallas_call x1, Pallas kernels: 36.2 us -> 32.3 us  [local(): pl.pallas_call(functools.partial(kernel, norm), name='galerkin', in_specs...]
where the time goes in v3:
time: 36.5 us; the launch traced here: 36.2 us
  Pallas kernels  32.3 us (88%)
  local copies, waits for them, and re-layouts  3.3 us (9%)
  between operations  0.64 us (2%)
    pallas_call x1, Pallas kernels, local(): pl.pallas_call(functools.partial(kernel, norm), name='galerkin', in_specs...  32.3 us
    unnamed x2, local copies, waits for them, and re-layouts  3.3 us

profile of v3, /device:TPU:0, one launch (start us, length us, event | category | flops | bytes accessed | tf_op | source)
XLA Modules:
  0.0 36.2 jit_solution(16125668445115711944)
XLA Ops:
  0.6 32.3 %galerkin.1 = (bf16[2,96,64,256]{3,2,1,0:T(8,128)(2,1)S(1)}, f32[2,2,256]{2,1,0:T(2,128)S(1)}) custom-call(s32[7,96]{1,0:T(8,128)} %bitcast.11, s32[4,8]{1,0:T(4,128)} %bitcast.12, s32[4,8]{1,0:T(4,128)} %bitcast.13, bf16[96,64,256]{2,1,0:T(8,128)(2,1)} %bitcast.8, f32[48,128]{1,0:T(8,128)} %bitcast.10, bf16[96,7,64,128]{3,2,1,0:T(8,128)(2,1)} %own_h.1, ...), custom_call_target="tpu_custom_call" | custom-call | flops 4700000256 | bytes 21000000 | tf_op jit(solution)/shard_map/galerkin/pallas_call | solution.py:392
  32.9 2.7 %copy.11 = bf16[2,6144,256]{2,1,0:T(8,128)(2,1)} copy(bf16[2,6144,256]{2,1,0:T(8,128)(2,1)S(1)} %bitcast.7) | data formatting | bytes 12582912
  35.6 0.6 %copy.12 = f32[2,2,256]{2,1,0:T(2,128)} copy(f32[2,2,256]{2,1,0:T(2,128)S(1)} %get-tuple-element.7) | data formatting | bytes 8192

commit v4 on v3

--- a/solution.py
+++ b/solution.py
@@ -35,20 +35,21 @@
 
 
 AROUND = ((1, 0, 0), (3, 0, 0), (0, 1, 0), (0, 3, 0), (0, 0, 1), (0, 0, 3))
-ROUNDS = (AROUND, ((0, 3, 1), (0, 1, 1)), ((0, 3, 2), (2, 0, 0)))
+ROUNDS = (AROUND, ((2, 0, 0), (0, 2, 0)), ((2, 1, 0), (0, 0, 2)))
 ORDER = (2, 3, 0, 1)
 HALF = NB // 2
+DETOUR = 2
 
 
 def kernel(
     norm,
     own_cols_h, border_cols_h, border_rows_h, basis_h, volume_h, own_h, border_h,
-    applied_out, reduced_out,
+    applied_out, recv_h,
     own_cols, border_cols, border_rows, volume,
-    own, basis, sums, volb, send_rows, send_b, recv_rows, recv_a, recv_b, relay_a, relay_b, table_v, table,
-    w_chunk, w_slot, part, q, pair, h, recv_h,
+    own, basis, sums, volb, send_rows, send_b, recv_rows, recv_a, recv_b, relay_a, relay_b, side_a, side_b, table_v, table,
+    w_chunk, w_slot, part, q, pair, h,
     own_sem, basis_sem, small_sem, table_sem, rows_ss, rows_rs, a_ss, a_rs, b_ss, b_rs,
-    in_ss, in_rs, out_ss, pair_ss, pair_rs, all_sem, known,
+    in_ss, in_rs, out_ss, side_ss, side_rs, side_out_ss, pair_ss, pair_rs, all_sem, known,
 ):
     s, c = lax.axis_index("stream"), lax.axis_index("cross")
     x, y, z = chip = ((c // 2) % 2 * 2 + s // 4, s % 4, c // 4)
@@ -70,6 +71,11 @@
     ]
     lands = (0, 1, jnp.where(s == 3, 3, 2), jnp.where(s == 5, 2, 3))
     corners = ((2, 3, 0, 4), (3, 4, 7, 3))
+    beside = (s + 1 - 2 * (s % 2), c + 1 - 2 * core)
+    outer = jnp.logical_or(s % 4 == 0, s % 4 == 3)
+    detours = tuple(jnp.logical_and(jnp.logical_and(outer, core == 1 - d), sides[d][0]) for d in range(2))
+    held_back = (False, False, s % 4 == 0, s % 4 == 3)
+    passes_on = jnp.logical_and(jnp.logical_not(outer), jnp.where(core == 0, c < 14, c > 1))
 
     small_copies = [
         pltpu.make_async_copy(source, landing, small_sem.at[i])
@@ -93,6 +99,7 @@
             pl.semaphore_signal(barrier, inc=1, device_id=target, device_id_type=MESH)
     pl.semaphore_signal(barrier, inc=1, device_id=mate, device_id_type=MESH)
 
+    pl.semaphore_signal(barrier, inc=1, device_id=beside, device_id_type=MESH)
     for step in AROUND:
         pl.semaphore_signal(barrier, inc=1, device_id=ident(moved(chip, *step), core), device_id_type=MESH)
 
@@ -106,90 +113,121 @@
             recv_a[d] = jnp.zeros((NB, BS, 2 * BS), BF16)
             recv_b[d] = jnp.zeros((NB, BS, MODES), BF16)
 
+    greeted = sum(jnp.where(may_receive, 1, 0) for _, _, may_receive in sides)
+    pl.semaphore_wait(barrier, greeted + 2 + len(AROUND))
+
+    def rows_copy(d, land):
+        return pltpu.make_async_remote_copy(
+            send_rows.at[d], recv_rows.at[land], rows_ss.at[d], rows_rs.at[land],
+            device_id=sides[d][1], device_id_type=MESH,
+        )
+
+    def half_copies(d, half, land, count=HALF):
+        blocks = pl.ds(half * HALF, count)
+        return (
+            pltpu.make_async_remote_copy(
+                border_h.at[ORDER[d], blocks], recv_a.at[land, blocks], a_ss.at[d, half], a_rs.at[land, half],
+                device_id=sides[d][1], device_id_type=MESH,
+            ),
+            pltpu.make_async_remote_copy(
+                send_b.at[d, blocks], recv_b.at[land, blocks], b_ss.at[d, half], b_rs.at[land, half],
+                device_id=sides[d][1], device_id_type=MESH,
+            ),
+        )
+
+    def corner_copies(d, corner, k):
+        return (
+            pltpu.make_async_remote_copy(
+                border_h.at[ORDER[d], HALF + k], relay_a.at[k], in_ss.at[0, k], in_rs.at[0, k],
+                device_id=(corner, c), device_id_type=MESH,
+            ),
+            pltpu.make_async_remote_copy(
+                send_b.at[d, HALF + k], relay_b.at[k], in_ss.at[1, k], in_rs.at[1, k],
+                device_id=(corner, c), device_id_type=MESH,
+            ),
+        )
+
+    def side_copies(d, k):
+        return (
+            pltpu.make_async_remote_copy(
+                border_h.at[ORDER[d], NB - DETOUR + k], side_a.at[k], side_ss.at[0, k], side_rs.at[0, k],
+                device_id=beside, device_id_type=MESH,
+            ),
+            pltpu.make_async_remote_copy(
+                send_b.at[d, NB - DETOUR + k], side_b.at[k], side_ss.at[1, k], side_rs.at[1, k],
+                device_id=beside, device_id_type=MESH,
+            ),
+        )
+
+    def side_onward_copies(k):
+        target = (beside[0], c + 2 - 4 * core)
+        return (
+            pltpu.make_async_remote_copy(
+                side_a.at[k], recv_a.at[core, NB - DETOUR + k], side_out_ss.at[0, k], a_rs.at[core, 1],
+                device_id=target, device_id_type=MESH,
+            ),
+            pltpu.make_async_remote_copy(
+                side_b.at[k], recv_b.at[core, NB - DETOUR + k], side_out_ss.at[1, k], b_rs.at[core, 1],
+                device_id=target, device_id_type=MESH,
+            ),
+        )
+
+    def onward_copies(receiver, k):
+        return (
+            pltpu.make_async_remote_copy(
+                relay_a.at[k], recv_a.at[3, HALF + k], out_ss.at[0, k], a_rs.at[3, 1],
+                device_id=(receiver, c), device_id_type=MESH,
+            ),
+            pltpu.make_async_remote_copy(
+                relay_b.at[k], recv_b.at[3, HALF + k], out_ss.at[1, k], b_rs.at[3, 1],
+                device_id=(receiver, c), device_id_type=MESH,
+            ),
+        )
+
+    by_corner = {d: (sender, corner) for d, sender, corner, _ in corners}
+
+    def send(d, which):
+        if d in by_corner:
+            sender, corner = by_corner[d]
+            special = s == sender
+
+            @pl.when(special)
+            def _():
+                for k in range(HALF):
+                    corner_copies(d, corner, k)[which].start()
+        else:
+            special = detours[d]
+
+            @pl.when(special)
+            def _():
+                for k in range(DETOUR):
+                    side_copies(d, k)[which].start()
+                half_copies(d, 1, lands[d], HALF - DETOUR)[which].start()
+
+        now = jnp.logical_and(sides[d][0], jnp.logical_not(held_back[d]))
+
+        @pl.when(now)
+        def _():
+            half_copies(d, 0, lands[d])[which].start()
+
+        @pl.when(jnp.logical_and(now, jnp.logical_not(special)))
+        def _():
+            half_copies(d, 1, lands[d])[which].start()
+
+    for d in (0, 1, 2, 3):
+        send(d, 0)
     small_copies[1].wait()
     for d in range(4):
         for n in range(NB):
             send_rows[d, pl.ds(n, 1), :] = jnp.full((1, 128), border_rows[ORDER[d], n], I32)
-    greeted = sum(jnp.where(may_receive, 1, 0) for _, _, may_receive in sides)
-    pl.semaphore_wait(barrier, greeted + 1 + len(AROUND))
-
-    def rows_copy(d, land):
-        return pltpu.make_async_remote_copy(
-            send_rows.at[d], recv_rows.at[land], rows_ss.at[d], rows_rs.at[land],
-            device_id=sides[d][1], device_id_type=MESH,
-        )
-
-    def half_copies(d, half, land):
-        blocks = pl.ds(half * HALF, HALF)
-        return (
-            pltpu.make_async_remote_copy(
-                border_h.at[ORDER[d], blocks], recv_a.at[land, blocks], a_ss.at[d, half], a_rs.at[land, half],
-                device_id=sides[d][1], device_id_type=MESH,
-            ),
-            pltpu.make_async_remote_copy(
-                send_b.at[d, blocks], recv_b.at[land, blocks], b_ss.at[d, half], b_rs.at[land, half],
-                device_id=sides[d][1], device_id_type=MESH,
-            ),
-        )
-
-    def corner_copies(d, corner, k):
-        return (
-            pltpu.make_async_remote_copy(
-                border_h.at[ORDER[d], HALF + k], relay_a.at[k], in_ss.at[0, k], in_rs.at[0, k],
-                device_id=(corner, c), device_id_type=MESH,
-            ),
-            pltpu.make_async_remote_copy(
-                send_b.at[d, HALF + k], relay_b.at[k], in_ss.at[1, k], in_rs.at[1, k],
-                device_id=(corner, c), device_id_type=MESH,
-            ),
-        )
-
-    def onward_copies(receiver, k):
-        return (
-            pltpu.make_async_remote_copy(
-                relay_a.at[k], recv_a.at[3, HALF + k], out_ss.at[0, k], a_rs.at[3, 1],
-                device_id=(receiver, c), device_id_type=MESH,
-            ),
-            pltpu.make_async_remote_copy(
-                relay_b.at[k], recv_b.at[3, HALF + k], out_ss.at[1, k], b_rs.at[3, 1],
-                device_id=(receiver, c), device_id_type=MESH,
-            ),
-        )
-
-    by_corner = {d: (sender, corner) for d, sender, corner, _ in corners}
-
-    def send(d, which):
+
         @pl.when(sides[d][0])
         def _():
-            half_copies(d, 0, lands[d])[which].start()
-
-        if d not in by_corner:
-            @pl.when(sides[d][0])
-            def _():
-                half_copies(d, 1, lands[d])[which].start()
-
-            return
-        sender, corner = by_corner[d]
-
-        @pl.when(s == sender)
-        def _():
-            for k in range(HALF):
-                corner_copies(d, corner, k)[which].start()
-
-        @pl.when(jnp.logical_and(sides[d][0], s != sender))
-        def _():
-            half_copies(d, 1, lands[d])[which].start()
-
-    for d in range(4):
-        @pl.when(sides[d][0])
-        def _():
             rows_copy(d, lands[d]).start()
 
-    for d in (2, 3, 0, 1):
-        send(d, 0)
     small_copies[0].wait()
     basis_copy.wait()
-    for d in (2, 3, 0, 1):
+    for d in (0, 1, 2, 3):
         for n in range(NB):
             send_b[d, n] = basis[border_cols[ORDER[d], n]]
         send(d, 1)
@@ -224,6 +262,29 @@
         def _():
             told(1)
             tell(2)
+
+        @pl.when(jnp.logical_and(step == 1, outer))
+        def _():
+            for d in range(2):
+                @pl.when(detours[d])
+                def _():
+                    for k in range(DETOUR):
+                        for copy in side_copies(d, k):
+                            copy.wait_send()
+            for d in (2, 3):
+                @pl.when(held_back[d])
+                def _():
+                    for half in range(2):
+                        for copy in half_copies(d, half, lands[d]):
+                            copy.start()
+
+        @pl.when(jnp.logical_and(step >= STEPS - DETOUR, passes_on))
+        def _():
+            k = step - (STEPS - DETOUR)
+            for copy in side_copies(0, k):
+                copy.wait_recv()
+            for copy in side_onward_copies(k):
+                copy.start()
 
         for j in range(UNROLL):
             i = step * UNROLL + j
@@ -344,44 +405,72 @@
             applied_out[0, i] = row[0:BS].astype(BF16)
             applied_out[1, i] = row[BS:2 * BS].astype(BF16)
 
+    for d, (may_send, _, _) in enumerate(sides):
+        @pl.when(may_send)
+        def _():
+            rows_copy(d, d).wait_send()
+            for copy in half_copies(d, 0, d):
+                copy.wait_send()
+
+        special = s == by_corner[d][0] if d in by_corner else detours[d]
+
+        @pl.when(jnp.logical_and(may_send, jnp.logical_not(special)))
+        def _():
+            for copy in half_copies(d, 1, d):
+                copy.wait_send()
+
+        if d not in by_corner:
+            @pl.when(special)
+            def _():
+                for copy in half_copies(d, 1, d, HALF - DETOUR):
+                    copy.wait_send()
+
+    @pl.when(passes_on)
+    def _():
+        for k in range(DETOUR):
+            for copy in side_onward_copies(k):
+                copy.wait_send()
+
+    for d, sender, corner, receiver in corners:
+        @pl.when(s == sender)
+        def _():
+            for k in range(HALF):
+                for copy in corner_copies(d, corner, k):
+                    copy.wait_send()
+
+        @pl.when(s == corner)
+        def _():
+            for k in range(HALF):
+                for copy in onward_copies(receiver, k):
+                    copy.wait_send()
+
     pltpu.make_async_remote_copy(
         h.at[pl.ds(1, 63)], recv_h.at[pl.ds(1, 63)], all_sem.at[0], all_sem.at[1], device_id=mate, device_id_type=MESH
     ).wait()
     recv_h[0] = h[x * 16 + y * 4 + z]
-    mine = recv_h[...].sum(axis=0)
+
+
+PIECES = 4
+
+
+def write_out(applied, tiles, applied_out, reduced_out, reduced, sems, sem):
+    copies = []
+    for term in range(2):
+        for piece in range(PIECES):
+            rows = pl.ds(piece * (ROWS // PIECES), ROWS // PIECES)
+            copies.append(pltpu.make_async_copy(applied.at[term, rows], applied_out.at[term, rows], sems.at[term, piece]))
+    for copy in copies:
+        copy.start()
+    mine = tiles[...].reshape(8, 8, 8, 128).sum(axis=1).sum(axis=0)
     for r in range(2):
         for lanes in range(4):
-            reduced_out[r, lanes // 2:lanes // 2 + 1, (lanes % 2) * 128:(lanes % 2 + 1) * 128] = mine[
+            reduced[r, lanes // 2:lanes // 2 + 1, (lanes % 2) * 128:(lanes % 2 + 1) * 128] = mine[
                 lanes * 2 + r:lanes * 2 + r + 1
             ]
-
-    for d, (may_send, _, _) in enumerate(sides):
-        @pl.when(may_send)
-        def _():
-            rows_copy(d, d).wait_send()
-            for copy in half_copies(d, 0, d):
-                copy.wait_send()
-
-        direct = may_send
-        if d in by_corner:
-            direct = jnp.logical_and(may_send, s != by_corner[d][0])
-
-        @pl.when(direct)
-        def _():
-            for copy in half_copies(d, 1, d):
-                copy.wait_send()
-    for d, sender, corner, receiver in corners:
-        @pl.when(s == sender)
-        def _():
-            for k in range(HALF):
-                for copy in corner_copies(d, corner, k):
-                    copy.wait_send()
-
-        @pl.when(s == corner)
-        def _():
-            for k in range(HALF):
-                for copy in onward_copies(receiver, k):
-                    copy.wait_send()
+    copies.append(pltpu.make_async_copy(reduced, reduced_out, sem))
+    copies[-1].start()
+    for copy in copies:
+        copy.wait()
 
 
 def local(basis, volume, own_blocks, own_cols, border_blocks, border_cols, border_rows):
@@ -389,14 +478,14 @@
     vmem = pl.BlockSpec(memory_space=pltpu.VMEM)
     anywhere = pl.BlockSpec(memory_space=pl.ANY)
     dma = pltpu.SemaphoreType.DMA
-    applied, reduced = pl.pallas_call(
+    applied, tiles = pl.pallas_call(
         functools.partial(kernel, norm),
         name="galerkin",
         in_specs=[anywhere] * 7,
         out_specs=[vmem, vmem],
         out_shape=[
             pltpu.VMEM((2, ROWS, BS, MODES), BF16),
-            pltpu.VMEM((2, 2, MODES), F32),
+            pltpu.VMEM((64, 8, 128), F32),
         ],
         scratch_shapes=[
             pltpu.SMEM((KOWN, ROWS), I32),
@@ -414,6 +503,8 @@
             pltpu.VMEM((4, NB, BS, MODES), BF16),
             pltpu.VMEM((HALF, BS, 2 * BS), BF16),
             pltpu.VMEM((HALF, BS, MODES), BF16),
+            pltpu.VMEM((DETOUR, BS, 2 * BS), BF16),
+            pltpu.VMEM((DETOUR, BS, MODES), BF16),
             pltpu.VMEM((8, 128), I32),
             pltpu.SMEM((8, 128), I32),
             pltpu.VMEM((PROJ, BS, 2 * MODES), BF16),
@@ -422,10 +513,10 @@
             pltpu.VMEM((2, 512, 128), F32),
             pltpu.VMEM((512, 128), F32),
             pltpu.VMEM((64, 8, 128), F32),
-            pltpu.VMEM((64, 8, 128), F32),
             dma((STEPS,)), dma(()), dma((4,)), dma(()),
             dma((4,)), dma((4,)), dma((4, 2)), dma((4, 2)), dma((4, 2)), dma((4, 2)),
             dma((2, HALF)), dma((2, HALF)), dma((2, HALF)),
+            dma((2, DETOUR)), dma((2, DETOUR)), dma((2, DETOUR)),
             dma((4,)), dma((4,)), dma((2,)), pltpu.SemaphoreType.REGULAR((len(ROUNDS),)),
         ],
         compiler_params=pltpu.CompilerParams(
@@ -441,6 +532,18 @@
         own_blocks,
         border_blocks[0],
     )
+    applied, reduced = pl.pallas_call(
+        write_out,
+        name="write_out",
+        in_specs=[pl.BlockSpec(memory_space=pltpu.VMEM)] * 2,
+        out_specs=[anywhere, anywhere],
+        out_shape=[
+            jax.ShapeDtypeStruct((2, ROWS, BS, MODES), BF16),
+            jax.ShapeDtypeStruct((2, 2, MODES), F32),
+        ],
+        scratch_shapes=[pltpu.VMEM((2, 2, MODES), F32), dma((2, PIECES)), dma(())],
+        compiler_params=pltpu.CompilerParams(vmem_limit_bytes=16 << 20),
+    )(applied, tiles)
     applied = applied.reshape(2, ROWS * BS, MODES)
     return applied, reduced
 

time: 36.5 us -> 35.2 us (0.964)
  local copies, waits for them, and re-layouts: 3.3 us -> 0 us
  Pallas kernels: 32.3 us -> 34.4 us
    unnamed x2 -> x0, local copies, waits for them, and re-layouts: 3.3 us -> none
    pallas_call x0 -> x1, Pallas kernels: none -> 2.75 us  [local(): pl.pallas_call(write_out, name='write_out', in_specs=[pl.BlockSpec(memory...]
    pallas_call x1, Pallas kernels: 32.3 us -> 31.7 us  [local(): pl.pallas_call(functools.partial(kernel, norm), name='galerkin', in_specs...]
where the time goes in v4:
time: 35.2 us; the launch traced here: 35.1 us
  Pallas kernels  34.4 us (98%)
  between operations  0.64 us (2%)
    pallas_call x1, Pallas kernels, local(): pl.pallas_call(functools.partial(kernel, norm), name='galerkin', in_specs...  31.7 us
    pallas_call x1, Pallas kernels, local(): pl.pallas_call(write_out, name='write_out', in_specs=[pl.BlockSpec(memory...  2.75 us

profile of v4, /device:TPU:0, one launch (start us, length us, event | category | flops | bytes accessed | tf_op | source)
XLA Modules:
  0.0 35.1 jit_solution(15055618844019590040)
XLA Ops:
  0.6 31.7 %galerkin.1 = (bf16[2,96,64,256]{3,2,1,0:T(8,128)(2,1)S(1)}, f32[64,8,128]{2,1,0:T(8,128)S(1)}) custom-call(s32[7,96]{1,0:T(8,128)} %bitcast.11, s32[4,8]{1,0:T(4,128)} %bitcast.12, s32[4,8]{1,0:T(4,128)} %bitcast.13, bf16[96,64,256]{2,1,0:T(8,128)(2,1)} %bitcast.8, f32[48,128]{1,0:T(8,128)} %bitcast.10, bf16[96,7,64,128]{3,2,1,0:T(8,128)(2,1)} %own_h.1, ...), custom_call_target="tpu_custom_call" | custom-call | flops 4700000256 | bytes 21000000 | tf_op jit(solution)/shard_map/galerkin/pallas_call | solution.py:481
  32.3 2.8 %write_out.1 = (bf16[2,96,64,256]{3,2,1,0:T(8,128)(2,1)}, f32[2,2,256]{2,1,0:T(2,128)}) custom-call(bf16[2,96,64,256]{3,2,1,0:T(8,128)(2,1)S(1)} %get-tuple-element.6.applied, f32[64,8,128]{2,1,0:T(8,128)S(1)} %get-tuple-element.7.tiles), custom_call_target="tpu_custom_call" | custom-call | tf_op jit(solution)/shard_map/write_out/pallas_call | solution.py:535

commit v5 on v4

--- a/solution.py
+++ b/solution.py
@@ -38,7 +38,7 @@
 ROUNDS = (AROUND, ((2, 0, 0), (0, 2, 0)), ((2, 1, 0), (0, 0, 2)))
 ORDER = (2, 3, 0, 1)
 HALF = NB // 2
-DETOUR = 2
+DETOUR = 1
 
 
 def kernel(
@@ -367,35 +367,30 @@
                     q[cc, pl.ds(at * 128 + lanes * 2 + r, 16, stride=8), :] = part[
                         lanes, pl.ds((at % 2) * 128 + (at // 2) * 4 + 2 * cc + r, 16, stride=8), :
                     ]
-    order = [(x + i) % 4 for i in (2, 1, 3, 0)]
-
     def pair_copy(i):
-        tiles = pl.ds(pl.multiple_of(order[i] * 128, 128), 128)
+        tiles = pl.ds(i * 128, 128)
         return pltpu.make_async_remote_copy(
             q.at[1 - core, tiles], pair.at[tiles], pair_ss.at[i], pair_rs.at[i], device_id=mate, device_id_type=MESH
-        )
-
-    def sum_copy(i, j):
-        from_it = (x - order[i] + 4) % 4 * 16 + (y - j // 4 + 4) % 4 * 4 + (z - j % 4 + 4) % 4
-        return from_it, pltpu.make_async_remote_copy(
-            h.at[order[i] * 16 + j], recv_h.at[from_it], all_sem.at[0], all_sem.at[1],
-            device_id=ident((order[i], j // 4, j % 4), core), device_id_type=MESH,
         )
 
     for i in range(4):
         pair_copy(i).start()
     for i in range(4):
         pair_copy(i).wait()
-        tiles = pl.ds(pl.multiple_of(order[i] * 128, 128), 128)
-        h[pl.ds(order[i] * 16, 16)] = (q[core, tiles] + pair[tiles]).reshape(16, 8, 128)
-
-        @pl.loop(0, 16)
-        def _(j):
-            from_it, copy = sum_copy(i, j)
-
-            @pl.when(from_it != 0)
-            def _():
-                copy.start()
+        tiles = pl.ds(i * 128, 128)
+        h[pl.ds(i * 16, 16)] = (q[core, tiles] + pair[tiles]).reshape(16, 8, 128)
+
+    @pl.loop(0, 64)
+    def _(k):
+        to = (k // 4 % 4, k % 4, k // 16)
+        from_it = (x - to[0] + 4) % 4 * 16 + (y - to[1] + 4) % 4 * 4 + (z - to[2] + 4) % 4
+
+        @pl.when(from_it != 0)
+        def _():
+            pltpu.make_async_remote_copy(
+                h.at[to[0] * 16 + to[1] * 4 + to[2]], recv_h.at[from_it], all_sem.at[0], all_sem.at[1],
+                device_id=ident(to, core), device_id_type=MESH,
+            ).start()
 
     @pl.loop(0, ROWS // 4)
     def _(step):

time: 35.2 us -> 34.1 us (0.969); the launches traced: 35.1 us -> 33.5 us
  Pallas kernels: 34.4 us -> 32.8 us
    pallas_call x1, Pallas kernels: 31.7 us -> 30.1 us  [local(): pl.pallas_call(functools.partial(kernel, norm), name='galerkin', in_specs...]
where the time goes in v5:
time: 34.1 us; the launch traced here: 33.5 us
  Pallas kernels  32.8 us (96%)
  between operations  0.64 us (2%)
    pallas_call x1, Pallas kernels, local(): pl.pallas_call(functools.partial(kernel, norm), name='galerkin', in_specs...  30.1 us
    pallas_call x1, Pallas kernels, local(): pl.pallas_call(write_out, name='write_out', in_specs=[pl.BlockSpec(memory...  2.75 us

profile of v5, /device:TPU:0, one launch (start us, length us, event | category | flops | bytes accessed | tf_op | source)
XLA Modules:
  0.0 33.5 jit_solution(12054955176159887142)
XLA Ops:
  0.6 30.1 %galerkin.1 = (bf16[2,96,64,256]{3,2,1,0:T(8,128)(2,1)S(1)}, f32[64,8,128]{2,1,0:T(8,128)S(1)}) custom-call(s32[7,96]{1,0:T(8,128)} %bitcast.11, s32[4,8]{1,0:T(4,128)} %bitcast.12, s32[4,8]{1,0:T(4,128)} %bitcast.13, bf16[96,64,256]{2,1,0:T(8,128)(2,1)} %bitcast.8, f32[48,128]{1,0:T(8,128)} %bitcast.10, bf16[96,7,64,128]{3,2,1,0:T(8,128)(2,1)} %own_h.1, ...), custom_call_target="tpu_custom_call" | custom-call | flops 4700000256 | bytes 21000000 | tf_op jit(solution)/shard_map/galerkin/pallas_call | solution.py:476
  30.7 2.8 %write_out.1 = (bf16[2,96,64,256]{3,2,1,0:T(8,128)(2,1)}, f32[2,2,256]{2,1,0:T(2,128)}) custom-call(bf16[2,96,64,256]{3,2,1,0:T(8,128)(2,1)S(1)} %get-tuple-element.6.applied, f32[64,8,128]{2,1,0:T(8,128)S(1)} %get-tuple-element.7.tiles), custom_call_target="tpu_custom_call" | custom-call | tf_op jit(solution)/shard_map/write_out/pallas_call | solution.py:530

commit v6 on v5

--- a/solution.py
+++ b/solution.py
@@ -263,7 +263,7 @@
             told(1)
             tell(2)
 
-        @pl.when(jnp.logical_and(step == 1, outer))
+        @pl.when(jnp.logical_and(step == 0, outer))
         def _():
             for d in range(2):
                 @pl.when(detours[d])

time: 34.1 us -> 34.1 us (level)
  no operation moved by 1% of the time
where the time goes in v6:
time: 34.1 us; the launch traced here: 33.5 us
  Pallas kernels  32.8 us (96%)
  between operations  0.64 us (2%)
    pallas_call x1, Pallas kernels, local(): pl.pallas_call(functools.partial(kernel, norm), name='galerkin', in_specs...  30.1 us
    pallas_call x1, Pallas kernels, local(): pl.pallas_call(write_out, name='write_out', in_specs=[pl.BlockSpec(memory...  2.75 us

profile of v6, /device:TPU:0, one launch (start us, length us, event | category | flops | bytes accessed | tf_op | source)
XLA Modules:
  0.0 33.5 jit_solution(2146792952237110547)
XLA Ops:
  0.6 30.1 %galerkin.1 = (bf16[2,96,64,256]{3,2,1,0:T(8,128)(2,1)S(1)}, f32[64,8,128]{2,1,0:T(8,128)S(1)}) custom-call(s32[7,96]{1,0:T(8,128)} %bitcast.11, s32[4,8]{1,0:T(4,128)} %bitcast.12, s32[4,8]{1,0:T(4,128)} %bitcast.13, bf16[96,64,256]{2,1,0:T(8,128)(2,1)} %bitcast.8, f32[48,128]{1,0:T(8,128)} %bitcast.10, bf16[96,7,64,128]{3,2,1,0:T(8,128)(2,1)} %own_h.1, ...), custom_call_target="tpu_custom_call" | custom-call | flops 4700000256 | bytes 21000000 | tf_op jit(solution)/shard_map/galerkin/pallas_call | solution.py:476
  30.7 2.8 %write_out.1 = (bf16[2,96,64,256]{3,2,1,0:T(8,128)(2,1)}, f32[2,2,256]{2,1,0:T(2,128)}) custom-call(bf16[2,96,64,256]{3,2,1,0:T(8,128)(2,1)S(1)} %get-tuple-element.6.applied, f32[64,8,128]{2,1,0:T(8,128)S(1)} %get-tuple-element.7.tiles), custom_call_target="tpu_custom_call" | custom-call | tf_op jit(solution)/shard_map/write_out/pallas_call | solution.py:530
